TPU v7x, 512 devices: a whole 4x4x16 slice. The times are simulated.
512 devices in a mesh: recv: 128 (over z, x, core), src: 4 (over y).
Axes of the slice: x: 4, y: 4, z: 16, core: 2. Of those that a mesh axis runs over, the one named last changes fastest.
Arguments:
- interactions: int32 [3, 49152], P(None, ('recv', 'src')), may hold values from 0 to 4095, as said below
- list_lengths: int32 [512], P(('recv', 'src')), may hold values from 48 to 96, as said below
- kernels: float32 [2048, 128, 16, 128], P(('recv', 'src')), may hold values from -0.0210316469 to 0.0210316469
- prestress: float32 [4096, 128], P(('recv', 'src')), may hold values from 2 to 3
- friction: float32 [4096, 128], P(('recv', 'src')), may hold values from 0.2 to 0.5
- load_rate: float32 [4096, 128], P(('recv', 'src')), may hold values from 0.04 to 0.08
Outputs:
- slip_rates: float32 [4096, 96, 128], P(('recv', 'src'))
Inputs may be any that keep to these rules, and one draw needn't show every extreme that they name: `interactions`: column e belongs to device block g = e // 96, g = i * 4 + j. Its receiver patch lies in [i * 4 * 8, (i + 1) * 4 * 8); its source patch p satisfies (p // 8) mod 4 == j; its owner is p // 32; its lag offset lies in [32, 48]. The entries of one block name at most 1 distinct source patches of one owner, and in every draw some owner supplies exactly that many distinct source patches to every block. `list_lengths`: some device's list is full and some device's list holds exactly half, in every draw.
All inputs are finite; a program needn't handle non-finite values.
Results may differ from a plain program's by a relative error of at most 0.0003.
Values sent between devices are 32-bit elements; how exact they have to be, the bound alone decides.
A program may use at most 128 MiB of HBM per device.

v0:
```python
import jax
import jax.numpy as jnp
from jax import lax
from jax.sharding import PartitionSpec as P

BLOCK = 32
BLOCKS = 3
NEWTON = 4


damping = 0.5


def inverse_sinh(values):
    magnitude = jnp.abs(values)
    result = jnp.log(magnitude + jnp.sqrt(1.0 + magnitude * magnitude))
    return jnp.where(values < 0, -result, result)


def friction_solve(drive, friction):
    rates = jnp.zeros_like(drive)
    for newton_step in range(NEWTON):
        misfit = damping * rates + friction * inverse_sinh(rates) - drive
        slope_now = damping + friction * lax.rsqrt(1.0 + rates * rates)
        rates = rates - misfit / slope_now
    return rates


def local(interactions, list_lengths, kernels, prestress, friction, load_rate):
    n_recv = lax.axis_size("recv")
    n_src = lax.axis_size("src")
    recv_idx = lax.axis_index("recv")
    src_idx = lax.axis_index("src")
    ent_count = interactions.shape[1]
    ker_count = kernels.shape[0]
    width = kernels.shape[1]
    lag_count = kernels.shape[2]
    patch_count = prestress.shape[0]
    per_kernel = ent_count // ker_count
    peer_cap = max(1, ent_count // (8 * n_recv))
    group_rows = n_src * patch_count
    receivers = interactions[0] - recv_idx * group_rows
    sources = interactions[1]
    owners = sources // group_rows
    local_patch = sources % patch_count
    delays = interactions[2]
    entry_numbers = jnp.arange(ent_count, dtype=jnp.int32)
    same_source = sources[None, :] == sources[:, None]
    first_of = jnp.min(jnp.where(same_source, entry_numbers[None, :], ent_count), axis=1)
    is_first = first_of == entry_numbers
    earlier = (
        (owners[None, :] == owners[:, None])
        & is_first[None, :]
        & (entry_numbers[None, :] < first_of[:, None])
    )
    ranks = jnp.sum(earlier.astype(jnp.int32), axis=1)
    slot_of = owners * peer_cap + ranks
    slot_ids = jnp.arange(n_recv * peer_cap, dtype=jnp.int32)
    filling = (slot_ids[:, None] == slot_of[None, :]) & is_first[None, :]
    wanted = jnp.sum(jnp.where(filling, local_patch[None, :], 0), axis=1)
    asked = lax.all_to_all(
        wanted.reshape(n_recv, peer_cap), "recv", split_axis=0, concat_axis=0, tiled=True
    ).reshape(-1)
    live = (entry_numbers < list_lengths[0]).astype(jnp.float32)
    patch_ids = jnp.arange(group_rows, dtype=jnp.int32)
    route_table = jnp.where(patch_ids[:, None] == receivers[None, :], live[None, :], 0.0)
    kernel_matrices = kernels.reshape(ker_count, width, lag_count * width)

    def cut_window(window, delay):
        return lax.dynamic_slice_in_dim(
            window, 2 * BLOCK - delay - (lag_count - 1), BLOCK + lag_count - 1, 0
        )

    def one_kernel(pair):
        segs, kern = pair
        pieces = [
            segs[:, lag_count - 1 - lag_idx : lag_count - 1 - lag_idx + BLOCK]
            for lag_idx in range(lag_count)
        ]
        stacked_rows = jnp.stack(pieces, axis=2).reshape(per_kernel * BLOCK, lag_count * width)
        return jnp.einsum("mk,rk->mr", stacked_rows, kern, precision=lax.Precision.HIGHEST)

    finished_blocks = []
    for block_idx in range(BLOCKS):
        if block_idx == 0:
            stress = jnp.zeros((patch_count, BLOCK, width), jnp.float32)
        else:
            recent = jnp.concatenate(finished_blocks[max(0, block_idx - 2) :], axis=1)
            span = recent.shape[1]
            outgoing = jnp.take(recent, asked, axis=0).reshape(n_recv, peer_cap, span, width)
            received = lax.all_to_all(outgoing, "recv", split_axis=0, concat_axis=0, tiled=True)
            picked = jnp.take(received.reshape(n_recv * peer_cap, span, width), slot_of, axis=0)
            windows = jnp.pad(picked, ((0, 0), (2 * BLOCK - span, 0), (0, 0)))
            segments = jax.vmap(cut_window)(windows, delays)
            grouped = segments.reshape(ker_count, per_kernel, BLOCK + lag_count - 1, width)
            stress_terms = lax.map(one_kernel, (grouped, kernel_matrices)).reshape(
                ent_count, BLOCK * width
            )
            summed = jnp.dot(route_table, stress_terms, precision=lax.Precision.HIGHEST)
            partial_terms = summed.reshape(group_rows, BLOCK, width)
            summed_all = lax.psum(partial_terms, "src")
            stress = lax.dynamic_slice_in_dim(summed_all, src_idx * patch_count, patch_count, 0)
        times = (block_idx * BLOCK + 1 + jnp.arange(BLOCK, dtype=jnp.int32)).astype(jnp.float32)
        drive = prestress[:, None, :] + load_rate[:, None, :] * times[None, :, None] + stress
        finished_blocks.append(friction_solve(drive, friction[:, None, :]))
    return jnp.concatenate(finished_blocks, axis=1)


def solution(mesh):
    in_specs = (
        P(None, ("recv", "src")),
        P(("recv", "src")),
        P(("recv", "src"), None, None, None),
        P(("recv", "src"), None),
        P(("recv", "src"), None),
        P(("recv", "src"), None),
    )
    out_specs = P(("recv", "src"), None, None)
    return jax.shard_map(local, mesh=mesh, in_specs=in_specs, out_specs=out_specs, check_vma=False)
```

profile of v0, /device:TPU:1, one launch (start us, length us, event | category | flops | bytes accessed | tf_op | source)
XLA Modules:
  0.0 746.6 jit_solution(15495887555175844307)
XLA Ops:
  9.3 20.4 %all-to-all-start = ((s32[128,1,1]{2,1,0:T(1,128)}), s32[128,1,1]{2,1,0:T(1,128)S(1)}, u32[]{:S(2)}, u32[]{:S(2)}) async-start(s32[128,1,1]{2,1,0:T(1,128)} %copy.163), calls=%async_computation | async-start | bytes 131072 | tf_op jit(solution)/shard_map/all_to_all | solution.py:61
  31.6 12.9 %all-to-all-done = s32[128,1,1]{2,1,0:T(1,128)S(1)} async-done(((s32[128,1,1]{2,1,0:T(1,128)}), s32[128,1,1]{2,1,0:T(1,128)S(1)}, u32[]{:S(2)}, u32[]{:S(2)}) %all-to-all-start) | async-done | bytes 544 | tf_op jit(solution)/shard_map/all_to_all | solution.py:61
  44.5 2.3 reduce
  49.3 5.7 all-to-all-start.1
  55.6 5.0 reshape.247
  61.8 90.0 %all-to-all-done.1 = f32[128,1,32,128]{3,2,1,0:T(8,128)S(1)} async-done(((f32[128,1,32,128]{3,2,1,0:T(8,128)}), f32[128,1,32,128]{3,2,1,0:T(8,128)S(1)}, u32[]{:S(2)}, u32[]{:S(2)}) %all-to-all-start.1) | async-done | bytes 2097184 | tf_op jit(solution)/shard_map/all_to_all | solution.py:91
  156.6 8.5 %gather_fusion.4 = f32[96,47,128]{2,0,1:T(8,128)} fusion(f32[96,64,128]{2,0,1:T(8,128)S(1)} %pad.5.clone, s32[96]{0:T(128)S(1)} %get-tuple-element.145), kind=kCustom, calls=%fused_computation.4 | custom fusion | bytes 4621440 | tf_op jit(solution)/shard_map/vmap()/gather | solution.py:70
  166.4 117.3 %while.20 = (s32[]{:T(128)}, f32[4,768,128]{2,1,0:T(8,128)}, f32[4,24,47,128]{3,1,0,2:T(8,128)}, f32[4,128,2048]{2,1,0:T(8,128)}, s32[]{:T(128)}) while((s32[]{:T(128)}, f32[4,768,128]{2,1,0:T(8,128)}, f32[4,24,47,128]{3,1,0,2:T(8,128)}, f32[4,128,2048]{2,1,0:T(8,128)}, s32[]{:T(128)}) %tuple.92), condition=%wide.region_4.5_spmd, body=%wide.region_3.4_spmd.sunk | while | flops 2415919104 | bytes 35210304 | solution.py:96
  169.7 16.2 %stack.104 = f32[24,32,16,128]{3,2,1,0:T(8,128)} concatenate(f32[24,32,1,128]{3,2,1,0:T(1,128)} %bitcast.321, f32[24,32,1,128]{3,2,1,0:T(1,128)} %bitcast.320, f32[24,32,1,128]{3,2,1,0:T(1,128)} %bitcast.319, f32[24,32,1,128]{3,2,1,0:T(1,128)} %bitcast.318, f32[24,32,1,128]{3,2,1,0:T(1,128)} %bitcast.317, f32[24,32,1,128]{3,2,1,0:T(1,128)} %bitcast.316, ...), dimensions={2} | concatenate | bytes 12582912 | tf_op jit(solution)/shard_map/while/body/eval_jaxpr/stack | solution.py:80
  185.9 9.9 %fusion.111 = f32[4,768,128]{2,1,0:T(8,128)} fusion(f32[4,768,128]{2,1,0:T(8,128)} %get-tuple-element.267, s32[]{:T(128)} %get-tuple-element.266, f32[96,8,16,128]{3,2,1,0:T(8,128)} %bitcast.304, f32[4,128,2048]{2,1,0:T(8,128)} %get-tuple-element.274), kind=kOutput, calls=%fused_computation.10.clone.1 | convolution fusion | flops 2415919104 | bytes 7734272 | tf_op jit(solution)/shard_map/while/body/eval_jaxpr/mk,rk->mr/dot_general | solution.py:81
  199.0 16.2 %stack.104 = f32[24,32,16,128]{3,2,1,0:T(8,128)} concatenate(f32[24,32,1,128]{3,2,1,0:T(1,128)} %bitcast.321, f32[24,32,1,128]{3,2,1,0:T(1,128)} %bitcast.320, f32[24,32,1,128]{3,2,1,0:T(1,128)} %bitcast.319, f32[24,32,1,128]{3,2,1,0:T(1,128)} %bitcast.318, f32[24,32,1,128]{3,2,1,0:T(1,128)} %bitcast.317, f32[24,32,1,128]{3,2,1,0:T(1,128)} %bitcast.316, ...), dimensions={2} | concatenate | bytes 12582912 | tf_op jit(solution)/shard_map/while/body/eval_jaxpr/stack | solution.py:80
  215.2 9.9 %fusion.111 = f32[4,768,128]{2,1,0:T(8,128)} fusion(f32[4,768,128]{2,1,0:T(8,128)} %get-tuple-element.267, s32[]{:T(128)} %get-tuple-element.266, f32[96,8,16,128]{3,2,1,0:T(8,128)} %bitcast.304, f32[4,128,2048]{2,1,0:T(8,128)} %get-tuple-element.274), kind=kOutput, calls=%fused_computation.10.clone.1 | convolution fusion | flops 2415919104 | bytes 7734272 | tf_op jit(solution)/shard_map/while/body/eval_jaxpr/mk,rk->mr/dot_general | solution.py:81
  228.3 16.2 %stack.104 = f32[24,32,16,128]{3,2,1,0:T(8,128)} concatenate(f32[24,32,1,128]{3,2,1,0:T(1,128)} %bitcast.321, f32[24,32,1,128]{3,2,1,0:T(1,128)} %bitcast.320, f32[24,32,1,128]{3,2,1,0:T(1,128)} %bitcast.319, f32[24,32,1,128]{3,2,1,0:T(1,128)} %bitcast.318, f32[24,32,1,128]{3,2,1,0:T(1,128)} %bitcast.317, f32[24,32,1,128]{3,2,1,0:T(1,128)} %bitcast.316, ...), dimensions={2} | concatenate | bytes 12582912 | tf_op jit(solution)/shard_map/while/body/eval_jaxpr/stack | solution.py:80
  244.5 9.9 %fusion.111 = f32[4,768,128]{2,1,0:T(8,128)} fusion(f32[4,768,128]{2,1,0:T(8,128)} %get-tuple-element.267, s32[]{:T(128)} %get-tuple-element.266, f32[96,8,16,128]{3,2,1,0:T(8,128)} %bitcast.304, f32[4,128,2048]{2,1,0:T(8,128)} %get-tuple-element.274), kind=kOutput, calls=%fused_computation.10.clone.1 | convolution fusion | flops 2415919104 | bytes 7734272 | tf_op jit(solution)/shard_map/while/body/eval_jaxpr/mk,rk->mr/dot_general | solution.py:81
  257.6 16.2 %stack.104 = f32[24,32,16,128]{3,2,1,0:T(8,128)} concatenate(f32[24,32,1,128]{3,2,1,0:T(1,128)} %bitcast.321, f32[24,32,1,128]{3,2,1,0:T(1,128)} %bitcast.320, f32[24,32,1,128]{3,2,1,0:T(1,128)} %bitcast.319, f32[24,32,1,128]{3,2,1,0:T(1,128)} %bitcast.318, f32[24,32,1,128]{3,2,1,0:T(1,128)} %bitcast.317, f32[24,32,1,128]{3,2,1,0:T(1,128)} %bitcast.316, ...), dimensions={2} | concatenate | bytes 12582912 | tf_op jit(solution)/shard_map/while/body/eval_jaxpr/stack | solution.py:80
  273.8 9.9 %fusion.111 = f32[4,768,128]{2,1,0:T(8,128)} fusion(f32[4,768,128]{2,1,0:T(8,128)} %get-tuple-element.267, s32[]{:T(128)} %get-tuple-element.266, f32[96,8,16,128]{3,2,1,0:T(8,128)} %bitcast.304, f32[4,128,2048]{2,1,0:T(8,128)} %get-tuple-element.274), kind=kOutput, calls=%fused_computation.10.clone.1 | convolution fusion | flops 2415919104 | bytes 7734272 | tf_op jit(solution)/shard_map/while/body/eval_jaxpr/mk,rk->mr/dot_general | solution.py:81
  287.1 51.5 %all-reduce.5.cloned.1.call-done = f32[32,32,128]{2,0,1:T(8,128)} async-done(((f32[32,32,128]{2,0,1:T(8,128)}), f32[32,32,128]{2,0,1:T(8,128)}) %all-reduce.5.cloned.1.call-update) | async-done | bytes 524304 | tf_op jit(solution)/shard_map/psum | solution.py:101
  340.1 2.8 gather_fusion.2
  342.8 2.5 fusion.24
  345.4 202.7 %all_to_all.25 = f32[128,1,64,128]{3,2,1,0:T(8,128)} all-to-all(f32[128,1,64,128]{3,2,1,0:T(8,128)S(1)} %fusion.24), channel_id=1, replica_groups=mesh['recv'=128,'src'=4] {'recv'}, dimensions={0} | all-to-all | bytes 8388608 | tf_op jit(solution)/shard_map/all_to_all | solution.py:91
  548.1 2.9 gather_fusion.3
  553.2 8.5 %gather_fusion.5 = f32[96,47,128]{2,0,1:T(8,128)} fusion(f32[96,64,128]{2,0,1:T(8,128)S(1)} %copy.171, s32[96]{0:T(128)S(1)} %get-tuple-element.145), kind=kCustom, calls=%fused_computation.5 | custom fusion | bytes 4621440 | tf_op jit(solution)/shard_map/vmap()/gather | solution.py:70
  562.9 117.4 %while.21 = (s32[]{:T(128)}, f32[4,768,128]{2,1,0:T(8,128)}, f32[4,24,47,128]{3,1,0,2:T(8,128)}, f32[4,128,2048]{2,1,0:T(8,128)}, s32[]{:T(128)}) while((s32[]{:T(128)}, f32[4,768,128]{2,1,0:T(8,128)}, f32[4,24,47,128]{3,1,0,2:T(8,128)}, f32[4,128,2048]{2,1,0:T(8,128)}, s32[]{:T(128)}) %tuple.91), condition=%wide.region_7.8_spmd, body=%wide.region_6.7_spmd.sunk | while | flops 2415919104 | bytes 35210304 | solution.py:96
  566.3 16.2 %stack.105 = f32[24,32,16,128]{3,2,1,0:T(8,128)} concatenate(f32[24,32,1,128]{3,2,1,0:T(1,128)} %bitcast.337, f32[24,32,1,128]{3,2,1,0:T(1,128)} %bitcast.336, f32[24,32,1,128]{3,2,1,0:T(1,128)} %bitcast.335, f32[24,32,1,128]{3,2,1,0:T(1,128)} %bitcast.334, f32[24,32,1,128]{3,2,1,0:T(1,128)} %bitcast.333, f32[24,32,1,128]{3,2,1,0:T(1,128)} %bitcast.332, ...), dimensions={2} | concatenate | bytes 12582912 | tf_op jit(solution)/shard_map/while/body/eval_jaxpr/stack | solution.py:80
  582.5 9.9 %fusion.115 = f32[4,768,128]{2,1,0:T(8,128)} fusion(f32[4,768,128]{2,1,0:T(8,128)} %get-tuple-element.282, s32[]{:T(128)} %get-tuple-element.281, f32[96,8,16,128]{3,2,1,0:T(8,128)} %bitcast.305, f32[4,128,2048]{2,1,0:T(8,128)} %get-tuple-element.289), kind=kOutput, calls=%fused_computation.20.clone.1 | convolution fusion | flops 2415919104 | bytes 7734272 | tf_op jit(solution)/shard_map/while/body/eval_jaxpr/mk,rk->mr/dot_general | solution.py:81
  595.6 16.2 %stack.105 = f32[24,32,16,128]{3,2,1,0:T(8,128)} concatenate(f32[24,32,1,128]{3,2,1,0:T(1,128)} %bitcast.337, f32[24,32,1,128]{3,2,1,0:T(1,128)} %bitcast.336, f32[24,32,1,128]{3,2,1,0:T(1,128)} %bitcast.335, f32[24,32,1,128]{3,2,1,0:T(1,128)} %bitcast.334, f32[24,32,1,128]{3,2,1,0:T(1,128)} %bitcast.333, f32[24,32,1,128]{3,2,1,0:T(1,128)} %bitcast.332, ...), dimensions={2} | concatenate | bytes 12582912 | tf_op jit(solution)/shard_map/while/body/eval_jaxpr/stack | solution.py:80
  611.8 9.9 %fusion.115 = f32[4,768,128]{2,1,0:T(8,128)} fusion(f32[4,768,128]{2,1,0:T(8,128)} %get-tuple-element.282, s32[]{:T(128)} %get-tuple-element.281, f32[96,8,16,128]{3,2,1,0:T(8,128)} %bitcast.305, f32[4,128,2048]{2,1,0:T(8,128)} %get-tuple-element.289), kind=kOutput, calls=%fused_computation.20.clone.1 | convolution fusion | flops 2415919104 | bytes 7734272 | tf_op jit(solution)/shard_map/while/body/eval_jaxpr/mk,rk->mr/dot_general | solution.py:81
  624.9 16.2 %stack.105 = f32[24,32,16,128]{3,2,1,0:T(8,128)} concatenate(f32[24,32,1,128]{3,2,1,0:T(1,128)} %bitcast.337, f32[24,32,1,128]{3,2,1,0:T(1,128)} %bitcast.336, f32[24,32,1,128]{3,2,1,0:T(1,128)} %bitcast.335, f32[24,32,1,128]{3,2,1,0:T(1,128)} %bitcast.334, f32[24,32,1,128]{3,2,1,0:T(1,128)} %bitcast.333, f32[24,32,1,128]{3,2,1,0:T(1,128)} %bitcast.332, ...), dimensions={2} | concatenate | bytes 12582912 | tf_op jit(solution)/shard_map/while/body/eval_jaxpr/stack | solution.py:80
  641.1 9.9 %fusion.115 = f32[4,768,128]{2,1,0:T(8,128)} fusion(f32[4,768,128]{2,1,0:T(8,128)} %get-tuple-element.282, s32[]{:T(128)} %get-tuple-element.281, f32[96,8,16,128]{3,2,1,0:T(8,128)} %bitcast.305, f32[4,128,2048]{2,1,0:T(8,128)} %get-tuple-element.289), kind=kOutput, calls=%fused_computation.20.clone.1 | convolution fusion | flops 2415919104 | bytes 7734272 | tf_op jit(solution)/shard_map/while/body/eval_jaxpr/mk,rk->mr/dot_general | solution.py:81
  654.2 16.2 %stack.105 = f32[24,32,16,128]{3,2,1,0:T(8,128)} concatenate(f32[24,32,1,128]{3,2,1,0:T(1,128)} %bitcast.337, f32[24,32,1,128]{3,2,1,0:T(1,128)} %bitcast.336, f32[24,32,1,128]{3,2,1,0:T(1,128)} %bitcast.335, f32[24,32,1,128]{3,2,1,0:T(1,128)} %bitcast.334, f32[24,32,1,128]{3,2,1,0:T(1,128)} %bitcast.333, f32[24,32,1,128]{3,2,1,0:T(1,128)} %bitcast.332, ...), dimensions={2} | concatenate | bytes 12582912 | tf_op jit(solution)/shard_map/while/body/eval_jaxpr/stack | solution.py:80
  670.4 9.9 %fusion.115 = f32[4,768,128]{2,1,0:T(8,128)} fusion(f32[4,768,128]{2,1,0:T(8,128)} %get-tuple-element.282, s32[]{:T(128)} %get-tuple-element.281, f32[96,8,16,128]{3,2,1,0:T(8,128)} %bitcast.305, f32[4,128,2048]{2,1,0:T(8,128)} %get-tuple-element.289), kind=kOutput, calls=%fused_computation.20.clone.1 | convolution fusion | flops 2415919104 | bytes 7734272 | tf_op jit(solution)/shard_map/while/body/eval_jaxpr/mk,rk->mr/dot_general | solution.py:81
  683.7 53.6 %all-reduce.7.cloned.1.call-done = f32[32,32,128]{2,0,1:T(8,128)} async-done(((f32[32,32,128]{2,0,1:T(8,128)}), f32[32,32,128]{2,0,1:T(8,128)}) %all-reduce.7.cloned.1.call-update) | async-done | bytes 524304 | tf_op jit(solution)/shard_map/psum | solution.py:101
  (117 shorter events, 52.9 us)
Async XLA Ops:
  9.3 35.2 %all-to-all-start = ((s32[128,1,1]{2,1,0:T(1,128)}), s32[128,1,1]{2,1,0:T(1,128)S(1)}, u32[]{:S(2)}, u32[]{:S(2)}) async-start(s32[128,1,1]{2,1,0:T(1,128)} %copy.163), calls=%async_computation | async-start | bytes 131072 | tf_op jit(solution)/shard_map/all_to_all | solution.py:61
  30.4 16.5 %copy-start.7 = (f32[8,128]{1,0:T(8,128)}, f32[8,128]{1,0:T(8,128)S(1)}, u32[]{:S(2)}) copy-start(f32[8,128]{1,0:T(8,128)S(1)} %get-tuple-element.139) | copy-start | bytes 12292
  30.4 16.5 %copy-start.10 = (f32[8,128]{1,0:T(8,128)}, f32[8,128]{1,0:T(8,128)S(1)}, u32[]{:S(2)}) copy-start(f32[8,128]{1,0:T(8,128)S(1)} %get-tuple-element.140) | copy-start | bytes 12292
  31.5 15.3 %copy-start = (f32[8,32,128]{2,0,1:T(8,128)}, f32[8,32,128]{2,0,1:T(8,128)S(1)}, u32[]{:S(2)}) copy-start(f32[8,32,128]{2,0,1:T(8,128)S(1)} %fusion.46) | copy-start | bytes 393220
  46.9 2.4 copy-start.13
  49.3 102.6 %all-to-all-start.1 = ((f32[128,1,32,128]{3,2,1,0:T(8,128)}), f32[128,1,32,128]{3,2,1,0:T(8,128)S(1)}, u32[]{:S(2)}, u32[]{:S(2)}) async-start(f32[128,1,32,128]{3,2,1,0:T(8,128)} %fusion.25), calls=%async_computation.1 | async-start | bytes 4194304 | tf_op jit(solution)/shard_map/all_to_all | solution.py:91
  55.0 283.6 %all-reduce.5.cloned.1.call-start = ((), (), s32[]{:S(2)}) async-start(), calls=%async_computation.3 | async-start | bytes 1048576 | tf_op jit(solution)/shard_map/psum | solution.py:101
  55.5 6.2 copy-start.15
  61.8 93.5 %copy-start.16 = (pred[96]{0:T(512)(128)(4,1)}, pred[96]{0:T(512)(128)(4,1)S(1)}, u32[]{:S(2)}) copy-start(pred[96]{0:T(512)(128)(4,1)S(1)} %compare_and_fusion.1) | copy-start | bytes 292
  283.7 1.6 copy-start.18
  283.7 54.8 %copy-start.5 = (f32[8,128]{1,0:T(8,128)S(1)}, f32[8,128]{1,0:T(8,128)}, u32[]{:S(2)}) copy-start(f32[8,128]{1,0:T(8,128)} %param.14) | copy-start | bytes 12292
  283.7 54.8 %copy-start.8 = (f32[8,128]{1,0:T(8,128)S(1)}, f32[8,128]{1,0:T(8,128)}, u32[]{:S(2)}) copy-start(f32[8,128]{1,0:T(8,128)} %copy-done.7) | copy-start | bytes 12292
  283.7 54.8 %copy-start.11 = (f32[8,128]{1,0:T(8,128)S(1)}, f32[8,128]{1,0:T(8,128)}, u32[]{:S(2)}) copy-start(f32[8,128]{1,0:T(8,128)} %copy-done.10) | copy-start | bytes 12292
  283.7 54.8 %copy-start.20 = (f32[8,128]{1,0:T(8,128)S(1)}, f32[8,128]{1,0:T(8,128)}, u32[]{:S(2)}) copy-start(f32[8,128]{1,0:T(8,128)} %param.15) | copy-start | bytes 12292
  283.7 54.8 %copy-start.22 = (f32[8,128]{1,0:T(8,128)S(1)}, f32[8,128]{1,0:T(8,128)}, u32[]{:S(2)}) copy-start(f32[8,128]{1,0:T(8,128)} %param.13) | copy-start | bytes 12292
  285.3 54.6 %copy-start.1 = (f32[8,32,128]{2,0,1:T(8,128)S(1)}, f32[8,32,128]{2,0,1:T(8,128)}, u32[]{:S(2)}) copy-start(f32[8,32,128]{2,0,1:T(8,128)} %copy-done) | copy-start | bytes 393220
  287.0 450.2 %all-reduce.7.cloned.1.call-start = ((), (), s32[]{:S(2)}) async-start(), calls=%async_computation.4 | async-start | bytes 1048576 | tf_op jit(solution)/shard_map/psum | solution.py:101
  340.0 2.9 copy-start.3
  340.0 2.8 copy-start.14
  548.1 2.9 copy-start.17
  680.3 1.6 copy-start.19
  680.3 57.0 %copy-start.6 = (f32[8,128]{1,0:T(8,128)S(1)}, f32[8,128]{1,0:T(8,128)}, u32[]{:S(2)}) copy-start(f32[8,128]{1,0:T(8,128)} %param.14) | copy-start | bytes 12292
  680.3 57.0 %copy-start.9 = (f32[8,128]{1,0:T(8,128)S(1)}, f32[8,128]{1,0:T(8,128)}, u32[]{:S(2)}) copy-start(f32[8,128]{1,0:T(8,128)} %copy-done.7) | copy-start | bytes 12292
  680.3 56.9 %copy-start.12 = (f32[8,128]{1,0:T(8,128)S(1)}, f32[8,128]{1,0:T(8,128)}, u32[]{:S(2)}) copy-start(f32[8,128]{1,0:T(8,128)} %copy-done.10) | copy-start | bytes 12292
  680.3 56.9 %copy-start.21 = (f32[8,128]{1,0:T(8,128)S(1)}, f32[8,128]{1,0:T(8,128)}, u32[]{:S(2)}) copy-start(f32[8,128]{1,0:T(8,128)} %param.15) | copy-start | bytes 12292
  680.3 56.9 %copy-start.23 = (f32[8,128]{1,0:T(8,128)S(1)}, f32[8,128]{1,0:T(8,128)}, u32[]{:S(2)}) copy-start(f32[8,128]{1,0:T(8,128)} %param.13) | copy-start | bytes 12292
  681.9 56.7 %copy-start.2 = (f32[8,32,128]{2,0,1:T(8,128)S(1)}, f32[8,32,128]{2,0,1:T(8,128)}, u32[]{:S(2)}) copy-start(f32[8,32,128]{2,0,1:T(8,128)} %copy-done) | copy-start | bytes 393220
  681.9 56.7 %copy-start.4 = (f32[8,32,128]{2,0,1:T(8,128)S(1)}, f32[8,32,128]{2,0,1:T(8,128)}, u32[]{:S(2)}) copy-start(f32[8,32,128]{2,0,1:T(8,128)} %copy-done.3) | copy-start | bytes 393220
Sparse Core Ops, SparseCore 0:
  287.2 51.3 all-reduce.4
  683.8 53.4 all-reduce.6
where the time goes:
time: 761 us; the launch traced here: 747 us
  waiting for transfers between devices  208 us (27%)
  blocking collectives  203 us (27%)
  local copies, waits for them, and re-layouts  196 us (26%)
  matrix products  82.8 us (11%)
  starting transfers between devices  26.7 us (4%)
  other arithmetic  15.5 us (2%)
  between operations  14.8 us (2%)
    all_to_all x1, blocking collectives, local(): lax.all_to_all(outgoing, 'recv', split_axis=0, concat_axis=0, tiled=True)  203 us
    another operation x8, local copies, waits for them, and re-layouts, one_kernel(): jnp.stack(pieces, axis=2).reshape(per_kernel * BLOCK, lag_count * width)  130 us
    psum x2, waiting for transfers between devices, local(): summed_all = lax.psum(partial_terms, 'src')  105 us
    all_to_all x1, waiting for transfers between devices, local(): lax.all_to_all(outgoing, 'recv', split_axis=0, concat_axis=0, tiled=True)  90 us
    dot_general x8, matrix products, one_kernel(): jnp.einsum('mk,rk->mr', stacked_rows, kern, precision=lax.Precision.HIGHEST)  79.5 us
    all_to_all x1, starting transfers between devices, local(): lax.all_to_all(wanted.reshape(n_recv, peer_cap), 'recv', split_axis=0, co...  20.4 us
    gather x2, local copies, waits for them, and re-layouts, cut_window(): lax.dynamic_slice_in_dim(window, 2 * BLOCK - delay - (lag_count - 1), BLO...  17 us
    slice x8, local copies, waits for them, and re-layouts, one_kernel(): segs[:, lag_count - 1 - lag_idx:lag_count - 1 - lag_idx + BLOCK]  15.4 us
  transfers between devices with their start and end apart: 4, of which 4 were waited for; matrix products, arithmetic and copies ran while one was open for 1% of the time, Pallas kernels for 0%

commit v1 on v0

v1 whole, which is shorter than its diff:
```python
import functools

import jax
import jax.numpy as jnp
from jax import lax
from jax.experimental import pallas as pl
from jax.experimental.pallas import tpu as pltpu
from jax.sharding import PartitionSpec as P

MESH = pl.DeviceIdType.MESH
F32 = jnp.float32
BF16 = jnp.bfloat16

PE = 128
LAGS = 16
BLOCK = 32
PATCH = 8
KER = 4
ENT = 24
NENT = KER * ENT
GRP = 8
SRC = 4
DAMP = 0.5
VMEM_LIMIT = 56 * 1024 * 1024
PAD = 6


def newton(drive, friction):
    v = drive / (DAMP + friction)
    for _ in range(3):
        square = 1.0 + v * v
        root = lax.rsqrt(square)
        mag = jnp.log(jnp.abs(v) + square * root)
        arc = jnp.where(v < 0, -mag, mag)
        slope = DAMP + friction * root
        v = v - (DAMP * v + friction * arc - drive) / slope
    return v


def split(value):
    high = value.astype(BF16)
    return high, (value - high.astype(F32)).astype(BF16)


def ask_kernel(
    n_z, inter_ref, pre_ref, fri_ref, load_ref, kern_ref,
    table_ref, weight_ref, wanted_ref,
    zbuf, req, asked, picked, kern_f32, req_s, req_r, z_s, z_r, x_s, x_r, loc,
):
    me, y = lax.axis_index("recv"), lax.axis_index("src")
    z, k_me = me // GRP, me % GRP
    barrier = pltpu.get_barrier_semaphore()
    for dz in range(1, n_z):
        pl.semaphore_signal(barrier, inc=1, device_id=(((z + dz) % n_z) * GRP + k_me, y), device_id_type=MESH)
    for dk in range(1, GRP):
        pl.semaphore_signal(barrier, inc=1, device_id=(z * GRP + (k_me + dk) % GRP, y), device_id_type=MESH)
    fetch = pltpu.make_async_copy(kern_ref, kern_f32, loc.at[0])
    fetch.start()
    zbuf[z, 0:8, :] = pre_ref[...]
    zbuf[z, 8:16, :] = fri_ref[...]
    zbuf[z, 16:24, :] = load_ref[...]
    row = inter_ref[1:2, :]
    eye = lax.broadcasted_iota(jnp.int32, (NENT, NENT), 0) == lax.broadcasted_iota(jnp.int32, (NENT, NENT), 1)
    column = jnp.sum(jnp.where(eye, jnp.broadcast_to(row, (NENT, NENT)), 0), axis=1, keepdims=True)
    owner = lax.shift_right_logical(column, 5)
    place = jnp.bitwise_and(column, PATCH - 1)
    hit = owner == lax.broadcasted_iota(jnp.int32, (NENT, n_z * GRP), 1)
    wanted = jnp.max(jnp.where(hit, place, 0), axis=0, keepdims=True)
    req[k_me] = jnp.broadcast_to(wanted, (8, n_z * GRP))
    pl.semaphore_wait(barrier, n_z - 1 + GRP - 1)
    sends = []
    for dk in range(1, GRP):
        sends.append(
            pltpu.make_async_remote_copy(
                src_ref=req.at[k_me], dst_ref=req.at[k_me], send_sem=req_s.at[dk - 1], recv_sem=req_r.at[dk - 1],
                device_id=(z * GRP + (k_me + dk) % GRP, y), device_id_type=MESH,
            )
        )
        sends[-1].start()
    zsends = []
    order = sorted(range(1, n_z), key=lambda d: -min(d, n_z - d))
    for dz in order:
        zsends.append(
            pltpu.make_async_remote_copy(
                src_ref=zbuf.at[z], dst_ref=zbuf.at[z], send_sem=z_s.at[dz - 1], recv_sem=z_r.at[dz - 1],
                device_id=(((z + dz) % n_z) * GRP + k_me, y), device_id_type=MESH,
            )
        )
        zsends[-1].start()
    for copy in sends:
        copy.wait()
    down = pltpu.make_async_copy(req, asked, loc.at[1])
    down.start()
    down.wait()
    for copy in zsends:
        copy.wait()

    def pick(k, carry):
        for zz in range(n_z):
            p = asked[k, 0, zz * GRP + k_me]
            for i in range(3):
                picked[k, i, zz : zz + 1, :] = zbuf[zz, pl.ds(8 * i + p, 1), :]
        return carry

    lax.fori_loop(0, GRP, pick, 0)
    xsends = []
    for dk in range(1, GRP):
        k = (k_me + dk) % GRP
        xsends.append(
            pltpu.make_async_remote_copy(
                src_ref=picked.at[k], dst_ref=table_ref.at[k_me], send_sem=x_s.at[dk - 1], recv_sem=x_r.at[dk - 1],
                device_id=(z * GRP + k, y), device_id_type=MESH,
            )
        )
        xsends[-1].start()
    table_ref[k_me] = picked[k_me]
    wanted_ref[...] = req[...]
    fetch.wait()

    def weights(i, carry):
        k, lag = i // LAGS, i % LAGS
        part = kern_f32[k, pl.ds(lag, PE, stride=LAGS), :]
        high, low = split(part.T)
        at = pl.ds(pl.multiple_of(lag * PE, PE), PE)
        weight_ref[k, at, 0:PE] = high
        weight_ref[k, at, PE : 2 * PE] = low
        return carry

    lax.fori_loop(0, KER * LAGS, weights, 0)
    for copy in xsends:
        copy.wait()


def ask(n_z, interactions, prestress, friction, load_rate, kernels):
    vm = pl.BlockSpec(memory_space=pltpu.VMEM)
    owners = n_z * GRP
    return pl.pallas_call(
        functools.partial(ask_kernel, n_z),
        out_shape=(
            jax.ShapeDtypeStruct((GRP, 3, n_z, PE), F32),
            jax.ShapeDtypeStruct((KER, LAGS * PE, 2 * PE), BF16),
            jax.ShapeDtypeStruct((GRP, 8, owners), jnp.int32),
        ),
        in_specs=[vm, vm, vm, vm, pl.BlockSpec(memory_space=pl.ANY)],
        out_specs=(vm, vm, vm),
        scratch_shapes=[
            pltpu.VMEM((n_z, 24, PE), F32),
            pltpu.VMEM((GRP, 8, owners), jnp.int32),
            pltpu.SMEM((GRP, 8, owners), jnp.int32),
            pltpu.VMEM((GRP, 3, n_z, PE), F32),
            pltpu.VMEM((KER, LAGS * PE, PE), F32),
            pltpu.SemaphoreType.DMA((GRP - 1,)),
            pltpu.SemaphoreType.DMA((GRP - 1,)),
            pltpu.SemaphoreType.DMA((n_z - 1,)),
            pltpu.SemaphoreType.DMA((n_z - 1,)),
            pltpu.SemaphoreType.DMA((GRP - 1,)),
            pltpu.SemaphoreType.DMA((GRP - 1,)),
            pltpu.SemaphoreType.DMA((2,)),
        ],
        compiler_params=pltpu.CompilerParams(
            collective_id=0, has_side_effects=True, vmem_limit_bytes=VMEM_LIMIT
        ),
        name="ask",
    )(interactions, prestress, friction, load_rate, kernels)


def put(high_ref, low_ref, start, left, right):
    at = pl.ds(pl.multiple_of(start, 2 * ENT), 2 * ENT)
    high_ref[at, 0:PE], low_ref[at, 0:PE] = split(left)
    high_ref[at, PE : 2 * PE], low_ref[at, PE : 2 * PE] = split(right)


def conv_tile(k, start_rows, pairs, high_ref, low_ref, weight_ref, rows):
    wide = len(pairs) * 2 * PE
    high = jnp.concatenate([high_ref[pl.ds(s, rows), :] for s in start_rows], axis=1)
    low = jnp.concatenate([low_ref[pl.ds(s, rows), :] for s in start_rows], axis=1)
    weight = weight_ref[k, 0:wide, :]
    both = jnp.dot(high, weight, preferred_element_type=F32)
    rest = jnp.dot(low, weight[:, 0:PE], preferred_element_type=F32)
    return both[:, 0:PE] + both[:, PE : 2 * PE] + rest


def route(k, inter_ref, length_ref, group_base, terms, sum_ref):
    live = jnp.clip(length_ref[0] - k * ENT, 0, ENT)

    def add(e, carry):
        q = inter_ref[0, k * ENT + e] - group_base
        sum_ref[q] += terms[pl.ds(e, BLOCK, stride=ENT), :]
        return carry

    lax.fori_loop(0, live, add, 0)


def first_kernel(
    n_z, inter_ref, length_ref, base_ref, table_ref, weight_ref, sum_ref, early_ref,
    rows, high, low, terms,
):
    sum_ref[...] = jnp.zeros_like(sum_ref)
    high[0 : PAD * ENT, :] = jnp.zeros((PAD * ENT, 2 * PE), BF16)
    low[0 : PAD * ENT, :] = jnp.zeros((PAD * ENT, 2 * PE), BF16)

    for k in range(KER):

        def fill(e, carry):
            p = inter_ref[1, k * ENT + e]
            owner = lax.shift_right_logical(p, 5)
            zz, kk = owner // GRP, owner % GRP
            for i in range(3):
                rows[i, pl.ds(e, 1), :] = table_ref[kk, i, pl.ds(zz, 1), :]
            delay = inter_ref[2, k * ENT + e]
            rows[3, pl.ds(e, 1), :] = jnp.full((1, PE), delay, jnp.int32).astype(F32)
            return carry

        lax.fori_loop(0, ENT, fill, 0)
        pre, fri, load, delay = rows[0], rows[1], rows[2], rows[3]

        def history(u):
            time = lax.convert_element_type(u + 17, F32) - delay
            v = newton(pre + load * (time + 1.0), fri)
            return jnp.where((time >= 0.0) & (time < 32.0), v, 0.0)

        def pair(keep, i, before):
            now, after = history(15 + 2 * i), history(16 + 2 * i)
            left = jnp.concatenate([now, after], axis=0)
            put(high, low, (PAD + 2 * i) * ENT, left, jnp.concatenate([before, now], axis=0))
            if keep:
                early_ref[k, pl.ds(pl.multiple_of((2 * i - 16) * ENT, 2 * ENT), 2 * ENT), :] = left
            return after

        last = lax.fori_loop(0, 8, functools.partial(pair, False), jnp.zeros((ENT, PE), F32))
        lax.fori_loop(8, 16, functools.partial(pair, True), last)

        def more(i, carry):
            both = jnp.concatenate([history(47 + 2 * i), history(48 + 2 * i)], axis=0)
            early_ref[k, pl.ds(pl.multiple_of((2 * i + 16) * ENT, 2 * ENT), 2 * ENT), :] = both
            return carry

        lax.fori_loop(0, 8, more, 0)

        for m in range(4):
            pairs = [j for j in range(8) if 2 * j <= 8 * m + 7]
            starts = [(8 * m - 2 * j + PAD) * ENT for j in pairs]
            terms[8 * m * ENT : (8 * m + 8) * ENT, :] = conv_tile(k, starts, pairs, high, low, weight_ref, 8 * ENT)
        route(k, inter_ref, length_ref, base_ref[0], terms, sum_ref)


def first(n_z, interactions, lengths, base, table, weight):
    vm = pl.BlockSpec(memory_space=pltpu.VMEM)
    sm = pl.BlockSpec(memory_space=pltpu.SMEM)
    return pl.pallas_call(
        functools.partial(first_kernel, n_z),
        out_shape=(
            jax.ShapeDtypeStruct((SRC * PATCH, BLOCK, PE), F32),
            jax.ShapeDtypeStruct((KER, 32 * ENT, PE), F32),
        ),
        in_specs=[sm, sm, sm, vm, vm],
        out_specs=(vm, vm),
        scratch_shapes=[
            pltpu.VMEM((4, ENT, PE), F32),
            pltpu.VMEM(((PAD + 32) * ENT, 2 * PE), BF16),
            pltpu.VMEM(((PAD + 32) * ENT, 2 * PE), BF16),
            pltpu.VMEM((BLOCK * ENT, PE), F32),
        ],
        compiler_params=pltpu.CompilerParams(vmem_limit_bytes=VMEM_LIMIT),
        name="first",
    )(interactions, lengths, base, table, weight)


def second_kernel(
    n_z, inter_ref, length_ref, base_ref, got_ref, weight_ref, early_ref, sum_ref,
    line, high, low, terms,
):
    sum_ref[...] = jnp.zeros_like(sum_ref)
    for k in range(KER):
        line[0 : 32 * ENT, :] = early_ref[k]
        line[32 * ENT : 48 * ENT, :] = jnp.zeros((16 * ENT, PE), F32)

        def place(e, carry):
            owner = lax.shift_right_logical(inter_ref[1, k * ENT + e], 5)
            delay = inter_ref[2, k * ENT + e]
            line[pl.ds((delay - 16) * ENT + e, BLOCK, stride=ENT), :] = got_ref[owner % GRP, owner // GRP]
            return carry

        lax.fori_loop(0, ENT, place, 0)

        def pair(i, carry):
            left = line[pl.ds(pl.multiple_of((2 * i + 2) * ENT, 2 * ENT), 2 * ENT), :]
            right = line[pl.ds(pl.multiple_of((2 * i + 1) * ENT, ENT), 2 * ENT), :]
            put(high, low, 2 * i * ENT, left, right)
            return carry

        lax.fori_loop(0, 23, pair, 0)
        for m in range(4):
            pairs = list(range(8))
            starts = [(8 * m + 14 - 2 * j) * ENT for j in pairs]
            terms[8 * m * ENT : (8 * m + 8) * ENT, :] = conv_tile(k, starts, pairs, high, low, weight_ref, 8 * ENT)
        route(k, inter_ref, length_ref, base_ref[0], terms, sum_ref)


def second(n_z, interactions, lengths, base, got, weight, early):
    vm = pl.BlockSpec(memory_space=pltpu.VMEM)
    sm = pl.BlockSpec(memory_space=pltpu.SMEM)
    return pl.pallas_call(
        functools.partial(second_kernel, n_z),
        out_shape=jax.ShapeDtypeStruct((SRC * PATCH, BLOCK, PE), F32),
        in_specs=[sm, sm, sm, vm, vm, vm],
        out_specs=vm,
        scratch_shapes=[
            pltpu.VMEM((64 * ENT, PE), F32),
            pltpu.VMEM((46 * ENT, 2 * PE), BF16),
            pltpu.VMEM((46 * ENT, 2 * PE), BF16),
            pltpu.VMEM((BLOCK * ENT, PE), F32),
        ],
        compiler_params=pltpu.CompilerParams(vmem_limit_bytes=VMEM_LIMIT),
        name="second",
    )(interactions, lengths, base, got, weight, early)


def start_strips(part_ref, parts, y_s, y_r):
    me, y = lax.axis_index("recv"), lax.axis_index("src")
    copies = []
    for dy in (2, 1, 3):
        to = (y + dy) % SRC
        copies.append(
            pltpu.make_async_remote_copy(
                src_ref=part_ref.at[pl.ds(to * PATCH, PATCH)], dst_ref=parts.at[dy - 1],
                send_sem=y_s.at[dy - 1], recv_sem=y_r.at[dy - 1],
                device_id=(me, to), device_id_type=MESH,
            )
        )
        copies[-1].start()
    return copies


def solve_patch(p, block, stress, pre_ref, fri_ref, load_ref):
    pre, fri, load = pre_ref[pl.ds(p, 1), :], fri_ref[pl.ds(p, 1), :], load_ref[pl.ds(p, 1), :]
    times = lax.broadcasted_iota(jnp.int32, (BLOCK, PE), 0).astype(F32) + float(block * BLOCK + 1)
    drive = pre + load * times
    if stress is not None:
        drive = drive + stress
    return newton(drive, jnp.broadcast_to(fri, (BLOCK, PE)))


def spread_kernel(
    n_z, part_ref, pre_ref, fri_ref, load_ref, asked, got_ref, rate_ref, *scratch
):
    half = n_z // 2
    parts, own, picked = scratch[:3]
    right = dict(enumerate(scratch[3 : 3 + half - 1], 1))
    left = dict(enumerate(scratch[3 + half - 1 : 3 + 2 * (half - 1)], 1))
    far = scratch[1 + 2 * half]
    y_s, y_r, r_s, r_r, l_s, l_r, x_s, x_r = scratch[2 + 2 * half :]
    right[half] = left[half] = far
    me, y = lax.axis_index("recv"), lax.axis_index("src")
    z, k_me = me // GRP, me % GRP
    to_right = (((z + 1) % n_z) * GRP + k_me, y)
    to_left = (((z + n_z - 1) % n_z) * GRP + k_me, y)
    barrier = pltpu.get_barrier_semaphore()
    for dy in range(1, SRC):
        pl.semaphore_signal(barrier, inc=1, device_id=(me, (y + dy) % SRC), device_id_type=MESH)
    for to in (to_right, to_left):
        pl.semaphore_signal(barrier, inc=1, device_id=to, device_id_type=MESH)
    for dk in range(1, GRP):
        pl.semaphore_signal(barrier, inc=1, device_id=(z * GRP + (k_me + dk) % GRP, y), device_id_type=MESH)
    pl.semaphore_wait(barrier, SRC - 1 + 2 + GRP - 1)

    strips = start_strips(part_ref, parts, y_s, y_r)
    for copy in strips:
        copy.wait_recv()

    def solve(p, carry):
        stress = part_ref[y * PATCH + p] + parts[0, p] + parts[1, p] + parts[2, p]
        v = solve_patch(p, 1, stress, pre_ref, fri_ref, load_ref)
        own[p] = v
        rate_ref[p] = v
        return carry

    lax.fori_loop(0, PATCH, solve, 0)

    def hop(source, target, h, s, send, recv, to):
        rows = pl.ds(h * (PATCH // 2), PATCH // 2)
        return pltpu.make_async_remote_copy(
            src_ref=source.at[rows], dst_ref=target.at[rows], send_sem=send.at[s - 1, h], recv_sem=recv.at[s - 1, h],
            device_id=to, device_id_type=MESH,
        )

    moves = {}

    def forward(s, h):
        for name, bufs, send, recv, to, far_half in (
            ("r", right, r_s, r_r, to_right, 0),
            ("l", left, l_s, l_r, to_left, 1),
        ):
            if s < half or (s == half and h == far_half):
                source = own if s == 1 else bufs[s - 1]
                moves[name, s, h] = hop(source, bufs[s], h, s, send, recv, to)
                moves[name, s, h].start()

    def serve(origin, buffer):
        for dk in range(1, GRP):
            k = (k_me + dk) % GRP
            picked[k, origin] = buffer[asked[k, 0, origin * GRP + k_me]]
            pltpu.make_async_remote_copy(
                src_ref=picked.at[k, origin], dst_ref=got_ref.at[k_me, origin],
                send_sem=x_s.at[dk - 1], recv_sem=x_r.at[dk - 1],
                device_id=(z * GRP + k, y), device_id_type=MESH,
            ).start()
        got_ref[k_me, origin] = buffer[asked[k_me, 0, origin * GRP + k_me]]

    for h in range(2):
        forward(1, h)
    serve(z, own)
    for s in range(1, half + 1):
        for h in range(2):
            for name in "rl":
                if (name, s, h) in moves:
                    moves[name, s, h].wait_recv()
            forward(s + 1, h)
        if s < half:
            serve((z + n_z - s) % n_z, right[s])
            serve((z + s) % n_z, left[s])
        else:
            serve((z + half) % n_z, far)
    for dk in range(1, GRP):
        k = (k_me + dk) % GRP
        pltpu.make_async_remote_copy(
            src_ref=picked.at[k], dst_ref=got_ref.at[k_me], send_sem=x_s.at[dk - 1], recv_sem=x_r.at[dk - 1],
            device_id=(z * GRP + k, y), device_id_type=MESH,
        ).wait()
    for copy in strips:
        copy.wait_send()
    for copy in moves.values():
        copy.wait_send()


def spread(n_z, part, prestress, friction, load_rate, asked):
    vm = pl.BlockSpec(memory_space=pltpu.VMEM)
    half = n_z // 2
    patches = (PATCH, BLOCK, PE)
    dma = pltpu.SemaphoreType.DMA
    return pl.pallas_call(
        functools.partial(spread_kernel, n_z),
        out_shape=(
            jax.ShapeDtypeStruct((GRP, n_z, BLOCK, PE), F32),
            jax.ShapeDtypeStruct(patches, F32),
        ),
        in_specs=[vm, vm, vm, vm, pl.BlockSpec(memory_space=pltpu.SMEM)],
        out_specs=(vm, vm),
        scratch_shapes=[
            pltpu.VMEM((SRC - 1,) + patches, F32),
            pltpu.VMEM(patches, F32),
            pltpu.VMEM((GRP, n_z, BLOCK, PE), F32),
            *[pltpu.VMEM(patches, F32) for _ in range(2 * (half - 1) + 1)],
            dma((SRC - 1,)), dma((SRC - 1,)),
            dma((half, 2)), dma((half, 2)), dma((half, 2)), dma((half, 2)),
            dma((GRP - 1,)), dma((GRP - 1,)),
        ],
        compiler_params=pltpu.CompilerParams(
            collective_id=1, has_side_effects=True, vmem_limit_bytes=VMEM_LIMIT
        ),
        name="spread",
    )(part, prestress, friction, load_rate, asked)


def finish_kernel(part_ref, pre_ref, fri_ref, load_ref, rate_ref, out_ref, parts, y_s, y_r):
    me, y = lax.axis_index("recv"), lax.axis_index("src")
    barrier = pltpu.get_barrier_semaphore()
    for dy in range(1, SRC):
        pl.semaphore_signal(barrier, inc=1, device_id=(me, (y + dy) % SRC), device_id_type=MESH)
    pl.semaphore_wait(barrier, SRC - 1)
    strips = start_strips(part_ref, parts, y_s, y_r)

    def early(p, carry):
        out_ref[p, 0:BLOCK] = solve_patch(p, 0, None, pre_ref, fri_ref, load_ref)
        out_ref[p, BLOCK : 2 * BLOCK] = rate_ref[p]
        return carry

    lax.fori_loop(0, PATCH, early, 0)
    for copy in strips:
        copy.wait()

    def late(p, carry):
        stress = part_ref[y * PATCH + p] + parts[0, p] + parts[1, p] + parts[2, p]
        out_ref[p, 2 * BLOCK :] = solve_patch(p, 2, stress, pre_ref, fri_ref, load_ref)
        return carry

    lax.fori_loop(0, PATCH, late, 0)


def finish(part, prestress, friction, load_rate, rates):
    vm = pl.BlockSpec(memory_space=pltpu.VMEM)
    dma = pltpu.SemaphoreType.DMA
    return pl.pallas_call(
        finish_kernel,
        out_shape=jax.ShapeDtypeStruct((PATCH, 3 * BLOCK, PE), F32),
        in_specs=[vm] * 5,
        out_specs=vm,
        scratch_shapes=[pltpu.VMEM((SRC - 1, PATCH, BLOCK, PE), F32), dma((SRC - 1,)), dma((SRC - 1,))],
        compiler_params=pltpu.CompilerParams(
            collective_id=2, has_side_effects=True, vmem_limit_bytes=VMEM_LIMIT
        ),
        name="finish",
    )(part, prestress, friction, load_rate, rates)


def local(interactions, list_lengths, kernels, prestress, friction, load_rate):
    n_z = lax.axis_size("recv") // GRP
    base = (lax.axis_index("recv") * (SRC * PATCH)).reshape(1)
    flat = kernels.reshape(KER, PE * LAGS, PE)
    table, weight, asked = ask(n_z, interactions, prestress, friction, load_rate, flat)
    part, early = first(n_z, interactions, list_lengths, base, table, weight)
    got, rates = spread(n_z, part, prestress, friction, load_rate, asked)
    part = second(n_z, interactions, list_lengths, base, got, weight, early)
    return finish(part, prestress, friction, load_rate, rates)


def solution(mesh):
    own = P(("recv", "src"))
    in_specs = (
        P(None, ("recv", "src")),
        own,
        P(("recv", "src"), None, None, None),
        P(("recv", "src"), None),
        P(("recv", "src"), None),
        P(("recv", "src"), None),
    )
    out_specs = P(("recv", "src"), None, None)
    return jax.shard_map(local, mesh=mesh, in_specs=in_specs, out_specs=out_specs, check_vma=False)
```

time: 761 us -> 142 us (0.19); the launches traced: 747 us -> 142 us
  waiting for transfers between devices: 208 us -> 0 us
  blocking collectives: 203 us -> 0 us
  local copies, waits for them, and re-layouts: 196 us -> 1.77 us
  Pallas kernels: 0 us -> 140 us
  matrix products: 82.8 us -> 0 us
  starting transfers between devices: 26.7 us -> 0 us
  other arithmetic: 15.5 us -> 0 us
  between operations: 14.8 us -> 0.68 us
    all_to_all x1 -> x0, blocking collectives: 203 us -> none  [local(): lax.all_to_all(outgoing, 'recv', split_axis=0, concat_axis=0, tiled=True)]
    pallas_call x0 -> x5, Pallas kernels: none -> 140 us  [the longest x1 56 us: spread(): pl.pallas_call(functools.partial(spread_kernel, n_z), out_shape=(jax.Shap...]
    another operation x10 -> x0, local copies, waits for them, and re-layouts: 132 us -> none  [the longest x8 130 us: one_kernel(): jnp.stack(pieces, axis=2).reshape(per_kernel * BLOCK, lag_count * width)]
    psum x2 -> x0, waiting for transfers between devices: 105 us -> none  [local(): summed_all = lax.psum(partial_terms, 'src')]
    all_to_all x2 -> x0, waiting for transfers between devices: 103 us -> none  [the longest x1 90 us: local(): lax.all_to_all(outgoing, 'recv', split_axis=0, concat_axis=0, tiled=True)]
    dot_general x10 -> x0, matrix products: 82.8 us -> none  [the longest x8 79.5 us: one_kernel(): jnp.einsum('mk,rk->mr', stacked_rows, kern, precision=lax.Precision.HIGHEST)]
    all_to_all x2 -> x0, starting transfers between devices: 26.1 us -> none  [the longest x1 20.4 us: local(): lax.all_to_all(wanted.reshape(n_recv, peer_cap), 'recv', split_axis=0, co...]
    gather x6 -> x0, local copies, waits for them, and re-layouts: 25.3 us -> none  [the longest x2 17 us: cut_window(): lax.dynamic_slice_in_dim(window, 2 * BLOCK - delay - (lag_count - 1), BLO...]
  transfers between devices with their start and end apart: 4 -> 0, of which waited for: 4 -> 0; matrix products, arithmetic and copies ran while one was open for 1% -> 0% of each run, Pallas kernels for 0% -> 0%
where the time goes in v1:
time: 142 us
  Pallas kernels  140 us (99%)
  local copies, waits for them, and re-layouts  1.77 us (1%)
    pallas_call x1, Pallas kernels, spread(): pl.pallas_call(functools.partial(spread_kernel, n_z), out_shape=(jax.Shap...  56 us
    pallas_call x1, Pallas kernels, ask(): pl.pallas_call(functools.partial(ask_kernel, n_z), out_shape=(jax.ShapeDt...  35.6 us
    pallas_call x1, Pallas kernels, first(): pl.pallas_call(functools.partial(first_kernel, n_z), out_shape=(jax.Shape...  20.9 us
    pallas_call x1, Pallas kernels, second(): pl.pallas_call(functools.partial(second_kernel, n_z), out_shape=jax.Shape...  14.7 us
    pallas_call x1, Pallas kernels, finish(): pl.pallas_call(finish_kernel, out_shape=jax.ShapeDtypeStruct((PATCH, 3 *...  12.5 us

profile of v1, /device:TPU:1, one launch (start us, length us, event | category | flops | bytes accessed | tf_op | source)
XLA Modules:
  0.0 142.1 jit_solution(8106844457280348588)
XLA Ops:
  0.7 35.6 %ask.1 = (f32[8,3,16,128]{3,2,1,0:T(8,128)}, bf16[4,2048,256]{2,1,0:T(8,128)(2,1)}, s32[8,8,128]{2,1,0:T(8,128)}) custom-call(s32[3,96]{1,0:T(4,128)} %inter_ref.5, f32[8,128]{1,0:T(8,128)} %pre_ref.5, f32[8,128]{1,0:T(8,128)} %fri_ref.5, f32[8,128]{1,0:T(8,128)} %load_ref.5, f32[4,2048,128]{2,1,0:T(8,128)} %bitcast.2), custom_call_target="tpu_custom_call" | custom-call | tf_op jit(solution)/shard_map/ask/pallas_call | solution.py:137
  36.2 20.9 %first.1 = (f32[32,32,128]{2,1,0:T(8,128)}, f32[4,768,128]{2,1,0:T(8,128)}) custom-call(s32[3,96]{1,0:T(4,128)} %inter_ref.5, s32[1]{0:T(128)S(6)} %copy.8.length_ref, s32[1]{0:T(128)} %bitcast.base_ref, f32[8,3,16,128]{3,2,1,0:T(8,128)} %get-tuple-element.12.table_ref, bf16[4,2048,256]{2,1,0:T(8,128)(2,1)} %get-tuple-element.13.weight_ref), custom_call_target="tpu_custom_call" | custom-call | tf_op jit(solution)/shard_map/first/pallas_call | solution.py:250
  57.1 56.0 %spread.1 = (f32[8,16,32,128]{3,2,1,0:T(8,128)}, f32[8,32,128]{2,1,0:T(8,128)}) custom-call(f32[32,32,128]{2,1,0:T(8,128)} %get-tuple-element.14.part_ref, f32[8,128]{1,0:T(8,128)} %pre_ref.5, f32[8,128]{1,0:T(8,128)} %fri_ref.5, f32[8,128]{1,0:T(8,128)} %load_ref.5, s32[8,8,128]{2,1,0:T(8,128)} %get-tuple-element.15.asked), custom_call_target="tpu_custom_call" | custom-call | tf_op jit(solution)/shard_map/spread/pallas_call | solution.py:441
  113.2 14.7 %second.1.part_ref = f32[32,32,128]{2,1,0:T(8,128)} custom-call(s32[3,96]{1,0:T(4,128)} %inter_ref.5, s32[1]{0:T(128)S(6)} %copy.8.length_ref, s32[1]{0:T(128)} %bitcast.base_ref, f32[8,16,32,128]{3,2,1,0:T(8,128)} %get-tuple-element.16.got_ref, bf16[4,2048,256]{2,1,0:T(8,128)(2,1)} %get-tuple-element.13.weight_ref, f32[4,768,128]{2,1,0:T(8,128)} %get-tuple-element.17.early_ref), custom_call_target="tpu_custom_call" | custom-call | tf_op jit(solution)/shard_map/second/pallas_call | solution.py:303
  127.9 12.5 %finish.1 = f32[8,96,128]{2,1,0:T(8,128)} custom-call(f32[32,32,128]{2,1,0:T(8,128)} %second.1.part_ref, f32[8,128]{1,0:T(8,128)} %pre_ref.5, f32[8,128]{1,0:T(8,128)} %fri_ref.5, f32[8,128]{1,0:T(8,128)} %load_ref.5, f32[8,32,128]{2,1,0:T(8,128)} %get-tuple-element.18.rate_ref), custom_call_target="tpu_custom_call" | custom-call | tf_op jit(solution)/shard_map/finish/pallas_call | solution.py:493
  140.4 1.8 %copy.9 = f32[8,96,128]{2,1,0:T(8,128)} copy(f32[8,96,128]{2,1,0:T(8,128)} %finish.1) | data formatting | bytes 786432

commit v2 on v1

v2 whole, which is shorter than its diff:
```python
import functools

import jax
import jax.numpy as jnp
from jax import lax
from jax.experimental import pallas as pl
from jax.experimental.pallas import tpu as pltpu
from jax.sharding import PartitionSpec as P

MESH = pl.DeviceIdType.MESH
F32 = jnp.float32
BF16 = jnp.bfloat16

PE = 128
LAGS = 16
BLOCK = 32
PATCH = 8
KER = 4
ENT = 24
NENT = KER * ENT
GRP = 8
SRC = 4
DAMP = 0.5
VMEM_LIMIT = 56 * 1024 * 1024
WIDE = 3 * LAGS * PE // 2
HALF = BLOCK // 2
PAD = 6


def recip(x):
    r = pl.reciprocal(x, approx=True)
    return r * (2.0 - x * r)


def newton(drive, friction, start=None):
    size = jnp.abs(drive) if start is None else drive
    v = size * (recip(DAMP + friction) if start is None else start)
    for _ in range(3):
        square = 1.0 + v * v
        root = lax.rsqrt(square)
        arc = jnp.log(v + square * root)
        v = (size + friction * (root * v - arc)) * recip(DAMP + friction * root)
    return jnp.where(drive < 0, -v, v) if start is None else v


def split(value):
    high = value.astype(BF16)
    return high, (value - high.astype(F32)).astype(BF16)


def ask_kernel(
    n_z, inter_ref, pre_ref, fri_ref, load_ref, kern_ref,
    table_ref, weight_ref, wanted_ref,
    zbuf, req, asked, picked, kern_f32, weight, req_s, req_r, z_s, z_r, x_s, x_r, loc, out_s,
):
    me, y = lax.axis_index("recv"), lax.axis_index("src")
    z, k_me = me // GRP, me % GRP
    barrier = pltpu.get_barrier_semaphore()
    for dz in range(1, n_z):
        pl.semaphore_signal(barrier, inc=1, device_id=(((z + dz) % n_z) * GRP + k_me, y), device_id_type=MESH)
    for dk in range(1, GRP):
        pl.semaphore_signal(barrier, inc=1, device_id=(z * GRP + (k_me + dk) % GRP, y), device_id_type=MESH)
    fetch = pltpu.make_async_copy(kern_ref, kern_f32, loc.at[0])
    fetch.start()
    zbuf[z, 0:8, :] = pre_ref[...]
    zbuf[z, 8:16, :] = fri_ref[...]
    zbuf[z, 16:24, :] = load_ref[...]
    row = inter_ref[1:2, :]
    eye = lax.broadcasted_iota(jnp.int32, (NENT, NENT), 0) == lax.broadcasted_iota(jnp.int32, (NENT, NENT), 1)
    column = jnp.sum(jnp.where(eye, jnp.broadcast_to(row, (NENT, NENT)), 0), axis=1, keepdims=True)
    owner = lax.shift_right_logical(column, 5)
    place = jnp.bitwise_and(column, PATCH - 1)
    hit = owner == lax.broadcasted_iota(jnp.int32, (NENT, n_z * GRP), 1)
    wanted = jnp.max(jnp.where(hit, place, 0), axis=0, keepdims=True)
    req[k_me] = jnp.broadcast_to(wanted, (8, n_z * GRP))
    pl.semaphore_wait(barrier, n_z - 1 + GRP - 1)
    sends = []
    for dk in range(1, GRP):
        sends.append(
            pltpu.make_async_remote_copy(
                src_ref=req.at[k_me], dst_ref=req.at[k_me], send_sem=req_s.at[dk - 1], recv_sem=req_r.at[dk - 1],
                device_id=(z * GRP + (k_me + dk) % GRP, y), device_id_type=MESH,
            )
        )
        sends[-1].start()
    zsends = []
    order = sorted(range(1, n_z), key=lambda d: -min(d, n_z - d))
    for dz in order:
        zsends.append(
            pltpu.make_async_remote_copy(
                src_ref=zbuf.at[z], dst_ref=zbuf.at[z], send_sem=z_s.at[dz - 1], recv_sem=z_r.at[dz - 1],
                device_id=(((z + dz) % n_z) * GRP + k_me, y), device_id_type=MESH,
            )
        )
        zsends[-1].start()
    fetch.wait()

    def weights(k, carry):
        for lag in range(LAGS):
            high, low = split(kern_f32[k, pl.ds(lag, PE, stride=LAGS), :].T)
            weight[k, lag * PE : (lag + 1) * PE, 0:PE] = high
            weight[k, lag * PE : (lag + 1) * PE, PE : 2 * PE] = low
            pair = lag // 2
            at, side = LAGS * PE + (pair // 2 * 2 + lag % 2) * PE, (pair % 2) * PE
            weight[k, at : at + PE, side : side + PE] = high
        return carry

    lax.fori_loop(0, KER, weights, 0)
    store = pltpu.make_async_copy(weight, weight_ref, out_s)
    store.start()
    for copy in sends:
        copy.wait()
    for k in range(GRP):
        wanted_ref[k : k + 1, :] = req[k, 0:1, :]
    down = pltpu.make_async_copy(wanted_ref, asked, loc.at[1])
    down.start()
    down.wait()
    for copy in zsends:
        copy.wait()

    def pick(k, carry):
        for zz in range(n_z):
            p = asked[k, zz * GRP + k_me]
            for i in range(3):
                picked[k, i, zz : zz + 1, :] = zbuf[zz, pl.ds(8 * i + p, 1), :]
        return carry

    lax.fori_loop(0, GRP, pick, 0)
    xsends = []
    for dk in range(1, GRP):
        k = (k_me + dk) % GRP
        xsends.append(
            pltpu.make_async_remote_copy(
                src_ref=picked.at[k], dst_ref=table_ref.at[k_me], send_sem=x_s.at[dk - 1], recv_sem=x_r.at[dk - 1],
                device_id=(z * GRP + k, y), device_id_type=MESH,
            )
        )
        xsends[-1].start()
    table_ref[k_me] = picked[k_me]
    for copy in xsends:
        copy.wait()
    store.wait()


def ask(n_z, interactions, prestress, friction, load_rate, kernels):
    vm = pl.BlockSpec(memory_space=pltpu.VMEM)
    owners = n_z * GRP
    return pl.pallas_call(
        functools.partial(ask_kernel, n_z),
        out_shape=(
            jax.ShapeDtypeStruct((GRP, 3, n_z, PE), F32),
            jax.ShapeDtypeStruct((KER, WIDE, 2 * PE), BF16),
            jax.ShapeDtypeStruct((GRP, owners), jnp.int32),
        ),
        in_specs=[vm, vm, vm, vm, pl.BlockSpec(memory_space=pl.ANY)],
        out_specs=(vm, pl.BlockSpec(memory_space=pl.ANY), vm),
        scratch_shapes=[
            pltpu.VMEM((n_z, 24, PE), F32),
            pltpu.VMEM((GRP, 8, owners), jnp.int32),
            pltpu.SMEM((GRP, owners), jnp.int32),
            pltpu.VMEM((GRP, 3, n_z, PE), F32),
            pltpu.VMEM((KER, LAGS * PE, PE), F32),
            pltpu.VMEM((KER, WIDE, 2 * PE), BF16),
            pltpu.SemaphoreType.DMA((GRP - 1,)),
            pltpu.SemaphoreType.DMA((GRP - 1,)),
            pltpu.SemaphoreType.DMA((n_z - 1,)),
            pltpu.SemaphoreType.DMA((n_z - 1,)),
            pltpu.SemaphoreType.DMA((GRP - 1,)),
            pltpu.SemaphoreType.DMA((GRP - 1,)),
            pltpu.SemaphoreType.DMA((2,)),
            pltpu.SemaphoreType.DMA,
        ],
        compiler_params=pltpu.CompilerParams(
            collective_id=0, has_side_effects=True, vmem_limit_bytes=VMEM_LIMIT
        ),
        name="ask",
    )(interactions, prestress, friction, load_rate, kernels)


def history_of(k, rows):
    pre, fri, load, delay = rows[k, 0], rows[k, 1], rows[k, 2], rows[k, 3]
    start = recip(DAMP + fri)

    def history(ahead):
        time = lax.convert_element_type(ahead, F32) - delay
        v = newton(pre + load * (time + 1.0), fri, start)
        return jnp.where((time >= 0.0) & (time < 32.0), v, 0.0)

    return history


def put(k, high_ref, low_ref, start, left, right):
    at = pl.ds(pl.multiple_of(start, 2 * ENT), 2 * ENT)
    high_ref[k, at, 0:PE], low_ref[k, at, 0:PE] = split(left)
    high_ref[k, at, PE : 2 * PE], low_ref[k, at, PE : 2 * PE] = split(right)


def conv(k, half, offset, skip, high_ref, low_ref, weight_ref, carry_ref, terms):
    def stacked(ref, t, times, pairs):
        starts = [(t + 14 - 2 * j - offset) * ENT for j in pairs]
        return jnp.concatenate([ref[k, start : start + times * ENT, :] for start in starts], axis=1)

    base = LAGS * PE
    if half:
        carry = carry_ref[k]
    elif skip:
        carry = jnp.zeros((2 * ENT, PE), F32)
    else:
        rest = jnp.dot(stacked(low_ref, -2, 2, (0, 2, 4, 6)), weight_ref[k, base:, :], preferred_element_type=F32)
        carry = rest[:, PE:]
    for t in range(half * HALF, half * HALF + HALF, 8):
        pairs = [j for j in range(8) if not skip or 2 * j <= t + 7]
        evens = pairs[::2]
        both = jnp.dot(stacked(high_ref, t, 8, pairs), weight_ref[k, 0 : len(pairs) * 2 * PE, :], preferred_element_type=F32)
        rest = jnp.dot(
            stacked(low_ref, t, 8, evens), weight_ref[k, base : base + len(evens) * 2 * PE, :], preferred_element_type=F32
        )
        late = jnp.concatenate([carry, rest[: 6 * ENT, PE:]], axis=0)
        carry = rest[6 * ENT :, PE:]
        terms[k, t * ENT : (t + 8) * ENT, :] = both[:, :PE] + both[:, PE:] + (rest[:, :PE] + late)
    if not half:
        carry_ref[k] = carry


def routes(inter_ref, length):
    me = lax.axis_index("recv")
    shape = (SRC * PATCH, NENT)
    hit = jnp.broadcast_to(inter_ref[0:1, :], shape) == lax.broadcasted_iota(jnp.int32, shape, 0) + me * (SRC * PATCH)
    live = lax.broadcasted_iota(jnp.int32, shape, 1) < length
    return jnp.where(hit & live, 1.0, 0.0).astype(BF16)


def route(half, route_ref, terms, part_ref):
    def pair(i, carry):
        t = half * HALF + 2 * i
        rows = [
            jnp.concatenate([terms[k, pl.ds(pl.multiple_of((t + j) * ENT, 8), ENT), :] for k in range(KER)], axis=0)
            for j in range(2)
        ]
        high, low = split(jnp.concatenate(rows, axis=1))
        both = jnp.dot(route_ref[...], high, preferred_element_type=F32)
        both = both + jnp.dot(route_ref[...], low, preferred_element_type=F32)
        part_ref[pl.ds(2 * i, SRC * PATCH, stride=HALF), :] = both[:, :PE]
        part_ref[pl.ds(2 * i + 1, SRC * PATCH, stride=HALF), :] = both[:, PE:]
        return carry

    lax.fori_loop(0, HALF // 2, pair, 0, unroll=2)


def start_weights(weight_hbm, weight, sems):
    copies = [pltpu.make_async_copy(weight_hbm.at[k], weight.at[k], sems.at[k]) for k in range(KER)]
    for copy in copies:
        copy.start()
    return copies


def start_strips(part_ref, parts, send, recv):
    me, y = lax.axis_index("recv"), lax.axis_index("src")
    rows = PATCH * HALF
    copies = []
    for dy in (2, 1, 3):
        to = (y + dy) % SRC
        copies.append(
            pltpu.make_async_remote_copy(
                src_ref=part_ref.at[pl.ds(to * rows, rows)], dst_ref=parts.at[dy - 1],
                send_sem=send.at[dy - 1], recv_sem=recv.at[dy - 1],
                device_id=(me, to), device_id_type=MESH,
            )
        )
        copies[-1].start()
    return copies


def strip_sum(p, part_ref, parts):
    y = lax.axis_index("src")
    own = part_ref[pl.ds(pl.multiple_of((y * PATCH + p) * HALF, HALF), HALF), :]
    at = pl.ds(pl.multiple_of(p * HALF, HALF), HALF)
    return own + parts[0, at, :] + parts[1, at, :] + parts[2, at, :]


def solve_patch(p, time, count, stress, pre_ref, fri_ref, load_ref):
    pre, fri, load = pre_ref[pl.ds(p, 1), :], fri_ref[pl.ds(p, 1), :], load_ref[pl.ds(p, 1), :]
    times = lax.broadcasted_iota(jnp.int32, (count, PE), 0).astype(F32) + float(time + 1)
    drive = pre + load * times
    if stress is not None:
        drive = drive + stress
    return newton(drive, jnp.broadcast_to(fri, (count, PE)))


PEERS = (4, 3, 5, 2, 6, 7, 1)
CUTS = 2


def spread_kernel(
    n_z, inter_ref, inter_rows, length_ref, table_ref, weight_hbm, pre_ref, fri_ref, load_ref, asked,
    got_ref, rate_ref, early_ref, *scratch
):
    half = n_z // 2
    rows, weight, w_s, high, low, carry_ref, terms, route_ref, picked = scratch[:9]
    part, parts, own = scratch[9:11], scratch[11:13], scratch[13:15]
    rest = scratch[15:]
    right = {s: rest[2 * s - 2 : 2 * s] for s in range(1, half)}
    left = {s: rest[2 * (half + s) - 4 : 2 * (half + s) - 2] for s in range(1, half)}
    far = rest[4 * half - 4 : 4 * half - 2]
    y_s, y_r, r_s, r_r, l_s, l_r, x_s, x_r, loc = rest[4 * half - 2 :]
    right[half] = left[half] = far
    right[0] = left[0] = own
    me, y = lax.axis_index("recv"), lax.axis_index("src")
    z, k_me = me // GRP, me % GRP
    to_right = (((z + 1) % n_z) * GRP + k_me, y)
    to_left = (((z + n_z - 1) % n_z) * GRP + k_me, y)
    barrier = pltpu.get_barrier_semaphore()
    for dy in range(1, SRC):
        pl.semaphore_signal(barrier, inc=1, device_id=(me, (y + dy) % SRC), device_id_type=MESH)
    for to in (to_right, to_left):
        pl.semaphore_signal(barrier, inc=1, device_id=to, device_id_type=MESH)
    for dk in range(1, GRP):
        pl.semaphore_signal(barrier, inc=1, device_id=(z * GRP + (k_me + dk) % GRP, y), device_id_type=MESH)

    copies = start_weights(weight_hbm, weight, w_s)
    route_ref[...] = routes(inter_rows, length_ref[0])
    for k in range(KER):
        high[k, 0 : PAD * ENT, :] = jnp.zeros((PAD * ENT, 2 * PE), BF16)
        low[k, 0 : PAD * ENT, :] = jnp.zeros((PAD * ENT, 2 * PE), BF16)

        def fill(e, carry):
            owner = lax.shift_right_logical(inter_ref[1, k * ENT + e], 5)
            zz, kk = owner // GRP, owner % GRP
            for i in range(3):
                rows[k, i, pl.ds(e, 1), :] = table_ref[kk, i, pl.ds(zz, 1), :]
            delay = inter_ref[2, k * ENT + e]
            rows[k, 3, pl.ds(e, 1), :] = jnp.full((1, PE), delay, jnp.int32).astype(F32)
            return carry

        lax.fori_loop(0, ENT, fill, 0, unroll=8)
        history = history_of(k, rows)

        def pair(i, before):
            now, after = history(32 + 2 * i), history(33 + 2 * i)
            side = jnp.concatenate([now, after], axis=0)
            put(k, high, low, (PAD + 2 * i) * ENT, side, jnp.concatenate([before, now], axis=0))
            return after

        lax.fori_loop(0, 16, pair, jnp.zeros((ENT, PE), F32))

    strips = []
    for th in range(2):
        for k in range(KER):
            if th == 0:
                copies[k].wait()
            conv(k, th, 14 - PAD, True, high, low, weight, carry_ref, terms)
        route(th, route_ref, terms, part[th])
        if th == 0:
            pl.semaphore_wait(barrier, SRC - 1 + 2 + GRP - 1)
        strips.append(start_strips(part[th], parts[th], y_s.at[th], y_r.at[th]))

    moves = {}

    def forward(s, th, h):
        for name, bufs, send, recv, to in (("r", right, r_s, r_r, to_right), ("l", left, l_s, l_r, to_left)):
            if s < half or (s == half and (h < CUTS // 2) == (name == "r")):
                at = pl.ds(h * (PATCH // CUTS), PATCH // CUTS)
                moves[name, s, th, h] = pltpu.make_async_remote_copy(
                    src_ref=bufs[s - 1][th].at[at], dst_ref=bufs[s][th].at[at],
                    send_sem=send.at[s - 1, th * CUTS + h], recv_sem=recv.at[s - 1, th * CUTS + h],
                    device_id=to, device_id_type=MESH,
                )
                moves[name, s, th, h].start()

    def pick(origin, slot, buffers):
        for k in range(GRP):
            for th in range(2):
                picked[k, slot, th * HALF : (th + 1) * HALF] = buffers[th][asked[k, origin * GRP + k_me]]

    def to_peers(first, count):
        for dk in PEERS:
            k = (k_me + dk) % GRP
            pltpu.make_async_remote_copy(
                src_ref=picked.at[k, pl.ds(first, count)], dst_ref=got_ref.at[k_me, pl.ds(first, count)],
                send_sem=x_s.at[dk - 1], recv_sem=x_r.at[dk - 1],
                device_id=(z * GRP + k, y), device_id_type=MESH,
            ).start()

    def early(i):
        def one(k, carry):
            history = history_of(k, rows)
            for b in range(4 * i, 4 * i + 4, 2):
                early_ref[k, b * ENT : (b + 2) * ENT, :] = jnp.concatenate([history(b + 48), history(b + 49)], axis=0)
            return carry

        lax.fori_loop(0, KER, one, 0)

    for th in range(2):
        for copy in strips[th]:
            copy.wait_recv()

        def solve(p, carry):
            v = solve_patch(p, BLOCK + th * HALF, HALF, strip_sum(p, part[th], parts[th]), pre_ref, fri_ref, load_ref)
            own[th][p] = v
            rate_ref[p, th * HALF : (th + 1) * HALF] = v
            return carry

        lax.fori_loop(0, PATCH, solve, 0)
        for h in range(CUTS):
            forward(1, th, h)
    pick(z, 0, own)
    to_peers(0, 1)
    for s in range(1, half + 1):
        early(s - 1)
        for th in range(2):
            for h in range(CUTS):
                for name in "rl":
                    if (name, s, th, h) in moves:
                        moves[name, s, th, h].wait_recv()
                forward(s + 1, th, h)
        if s < half:
            pick((z + n_z - s) % n_z, 2 * s - 1, right[s])
            pick((z + s) % n_z, 2 * s, left[s])
            to_peers(2 * s - 1, 2)
        else:
            pick((z + half) % n_z, n_z - 1, far)
            to_peers(n_z - 1, 1)
    mine = pltpu.make_async_copy(picked.at[k_me], got_ref.at[k_me], loc)
    mine.start()
    for dk in range(1, GRP):
        k = (k_me + dk) % GRP
        pltpu.make_async_remote_copy(
            src_ref=picked.at[k], dst_ref=got_ref.at[k_me], send_sem=x_s.at[dk - 1], recv_sem=x_r.at[dk - 1],
            device_id=(z * GRP + k, y), device_id_type=MESH,
        ).wait()
    mine.wait()
    for copy in (*strips[0], *strips[1], *moves.values()):
        copy.wait_send()


def spread(n_z, interactions, lengths, table, weight, prestress, friction, load_rate, asked):
    vm = pl.BlockSpec(memory_space=pltpu.VMEM)
    sm = pl.BlockSpec(memory_space=pltpu.SMEM)
    hbm = pl.BlockSpec(memory_space=pl.ANY)
    half = n_z // 2
    dma = pltpu.SemaphoreType.DMA
    halves = pltpu.VMEM((PATCH, HALF, PE), F32)
    return pl.pallas_call(
        functools.partial(spread_kernel, n_z),
        out_shape=(
            jax.ShapeDtypeStruct((GRP, n_z, BLOCK, PE), F32),
            jax.ShapeDtypeStruct((PATCH, BLOCK, PE), F32),
            jax.ShapeDtypeStruct((KER, BLOCK * ENT, PE), F32),
        ),
        in_specs=[sm, vm, sm, vm, hbm, vm, vm, vm, sm],
        out_specs=(hbm, vm, vm),
        scratch_shapes=[
            pltpu.VMEM((KER, 4, ENT, PE), F32),
            *compute_scratch(PAD + 32),
            pltpu.VMEM((GRP, n_z, BLOCK, PE), F32),
            *strip_scratch(),
            halves, halves,
            *[halves for _ in range(2 * (2 * (half - 1) + 1))],
            dma((2, SRC - 1)), dma((2, SRC - 1)),
            *[dma((half, 2 * CUTS)) for _ in range(4)],
            dma((GRP - 1,)), dma((GRP - 1,)), dma,
        ],
        compiler_params=pltpu.CompilerParams(
            collective_id=1, has_side_effects=True, vmem_limit_bytes=VMEM_LIMIT
        ),
        name="spread",
    )(interactions, interactions, lengths, table, weight, prestress, friction, load_rate, asked)


def compute_scratch(blocks):
    return [
        pltpu.VMEM((KER, WIDE, 2 * PE), BF16),
        pltpu.SemaphoreType.DMA((KER,)),
        pltpu.VMEM((KER, blocks * ENT, 2 * PE), BF16),
        pltpu.VMEM((KER, blocks * ENT, 2 * PE), BF16),
        pltpu.VMEM((KER, 2 * ENT, PE), F32),
        pltpu.VMEM((KER, BLOCK * ENT, PE), F32),
        pltpu.VMEM((SRC * PATCH, NENT), BF16),
    ]


def strip_scratch():
    part = pltpu.VMEM((SRC * PATCH * HALF, PE), F32)
    parts = pltpu.VMEM((SRC - 1, PATCH * HALF, PE), F32)
    return [part, part, parts, parts]


def finish_kernel(
    n_z, inter_ref, inter_rows, length_ref, got_hbm, weight_hbm, early_ref, pre_ref, fri_ref, load_ref, rate_ref, out_ref,
    got_ref, loc, line, weight, w_s, high, low, carry_ref, terms, route_ref, part_a, part_b, parts_a, parts_b, y_s, y_r,
):
    me, y = lax.axis_index("recv"), lax.axis_index("src")
    z = me // GRP
    part, parts = (part_a, part_b), (parts_a, parts_b)
    barrier = pltpu.get_barrier_semaphore()
    for dy in range(1, SRC):
        pl.semaphore_signal(barrier, inc=1, device_id=(me, (y + dy) % SRC), device_id_type=MESH)
    fetch = pltpu.make_async_copy(got_hbm, got_ref.at[:, :, pl.ds(HALF, BLOCK)], loc)
    fetch.start()
    copies = start_weights(weight_hbm, weight, w_s)
    route_ref[...] = routes(inter_rows, length_ref[0])

    def clear(k, carry):
        got_ref[k, :, 0:HALF, :] = jnp.zeros((n_z, HALF, PE), F32)
        return carry

    lax.fori_loop(0, GRP, clear, 0)

    def known(p, carry):
        out_ref[p, 0:BLOCK] = solve_patch(p, 0, BLOCK, None, pre_ref, fri_ref, load_ref)
        out_ref[p, BLOCK : 2 * BLOCK] = rate_ref[p]
        return carry

    lax.fori_loop(0, PATCH, known, 0)
    fetch.wait()
    for k in range(KER):
        line[0 : 32 * ENT, :] = early_ref[k]
        line[32 * ENT : 48 * ENT, :] = jnp.zeros((16 * ENT, PE), F32)

        def place(e, carry):
            owner = lax.shift_right_logical(inter_ref[1, k * ENT + e], 5)
            delay = inter_ref[2, k * ENT + e]
            ahead = (owner // GRP - z + n_z) % n_z
            slot = jnp.where(ahead < n_z // 2, 2 * ahead, 2 * (n_z - ahead) - 1)
            line[pl.ds(16 * ENT + e, BLOCK, stride=ENT), :] += got_ref[owner % GRP, slot, pl.ds(jnp.clip(48 - delay, 0, HALF), BLOCK), :]
            return carry

        lax.fori_loop(0, ENT, place, 0, unroll=8)

        def pair(i, carry):
            left = line[pl.ds(pl.multiple_of((2 * i + 2) * ENT, 2 * ENT), 2 * ENT), :]
            right = line[pl.ds(pl.multiple_of((2 * i + 1) * ENT, ENT), 2 * ENT), :]
            put(k, high, low, 2 * i * ENT, left, right)
            return carry

        lax.fori_loop(0, 23, pair, 0)

    strips = []
    for th in range(2):
        for k in range(KER):
            if th == 0:
                copies[k].wait()
            conv(k, th, 0, False, high, low, weight, carry_ref, terms)
        route(th, route_ref, terms, part[th])
        if th == 0:
            pl.semaphore_wait(barrier, SRC - 1)
        strips.append(start_strips(part[th], parts[th], y_s.at[th], y_r.at[th]))
    for th in range(2):
        for copy in strips[th]:
            copy.wait()

        def solve(p, carry):
            at = pl.ds(2 * BLOCK + th * HALF, HALF)
            stress = strip_sum(p, part[th], parts[th])
            out_ref[p, at] = solve_patch(p, 2 * BLOCK + th * HALF, HALF, stress, pre_ref, fri_ref, load_ref)
            return carry

        lax.fori_loop(0, PATCH, solve, 0)


def finish(n_z, interactions, lengths, got, weight, early, prestress, friction, load_rate, rates):
    vm = pl.BlockSpec(memory_space=pltpu.VMEM)
    sm = pl.BlockSpec(memory_space=pltpu.SMEM)
    hbm = pl.BlockSpec(memory_space=pl.ANY)
    dma = pltpu.SemaphoreType.DMA
    return pl.pallas_call(
        functools.partial(finish_kernel, n_z),
        out_shape=jax.ShapeDtypeStruct((PATCH, 3 * BLOCK, PE), F32),
        in_specs=[sm, vm, sm, hbm, hbm, vm, vm, vm, vm, vm],
        out_specs=vm,
        scratch_shapes=[
            pltpu.VMEM((GRP, n_z, HALF + BLOCK, PE), F32),
            dma,
            pltpu.VMEM((48 * ENT, PE), F32),
            *compute_scratch(46),
            *strip_scratch(),
            dma((2, SRC - 1)), dma((2, SRC - 1)),
        ],
        compiler_params=pltpu.CompilerParams(
            collective_id=2, has_side_effects=True, vmem_limit_bytes=VMEM_LIMIT
        ),
        name="finish",
    )(interactions, interactions, lengths, got, weight, early, prestress, friction, load_rate, rates)


def local(interactions, list_lengths, kernels, prestress, friction, load_rate):
    n_z = lax.axis_size("recv") // GRP
    flat = kernels.reshape(KER, PE * LAGS, PE)
    own = (prestress, friction, load_rate)
    table, weight, asked = ask(n_z, interactions, *own, flat)
    got, rates, early = spread(n_z, interactions, list_lengths, table, weight, *own, asked)
    return finish(n_z, interactions, list_lengths, got, weight, early, *own, rates)


def solution(mesh):
    own = P(("recv", "src"))
    in_specs = (
        P(None, ("recv", "src")),
        own,
        P(("recv", "src"), None, None, None),
        P(("recv", "src"), None),
        P(("recv", "src"), None),
        P(("recv", "src"), None),
    )
    out_specs = P(("recv", "src"), None, None)
    return jax.shard_map(local, mesh=mesh, in_specs=in_specs, out_specs=out_specs, check_vma=False)
```

time: 142 us -> 115 us (0.81)
  Pallas kernels: 140 us -> 113 us
    pallas_call x3 -> x1, Pallas kernels: 48.1 us -> 21 us  [finish(): pl.pallas_call(functools.partial(finish_kernel, n_z), out_shape=jax.Shape...]
    pallas_call x1, Pallas kernels: 35.6 us -> 33.5 us  [ask(): pl.pallas_call(functools.partial(ask_kernel, n_z), out_shape=(jax.ShapeDt...]
    pallas_call x1, Pallas kernels: 56 us -> 58 us  [spread(): pl.pallas_call(functools.partial(spread_kernel, n_z), out_shape=(jax.Shap...]
where the time goes in v2:
time: 115 us
  Pallas kernels  113 us (98%)
  local copies, waits for them, and re-layouts  1.77 us (2%)
    pallas_call x1, Pallas kernels, spread(): pl.pallas_call(functools.partial(spread_kernel, n_z), out_shape=(jax.Shap...  58 us
    pallas_call x1, Pallas kernels, ask(): pl.pallas_call(functools.partial(ask_kernel, n_z), out_shape=(jax.ShapeDt...  33.5 us
    pallas_call x1, Pallas kernels, finish(): pl.pallas_call(functools.partial(finish_kernel, n_z), out_shape=jax.Shape...  21 us

profile of v2, /device:TPU:1, one launch (start us, length us, event | category | flops | bytes accessed | tf_op | source)
XLA Modules:
  0.0 115.0 jit_solution(8079268791378857430)
XLA Ops:
  0.7 33.5 %ask.1 = (f32[8,3,16,128]{3,2,1,0:T(8,128)}, bf16[4,3072,256]{2,1,0:T(8,128)(2,1)}, s32[8,128]{1,0:T(8,128)}) custom-call(s32[3,96]{1,0:T(4,128)} %inter_rows.3, f32[8,128]{1,0:T(8,128)} %pre_ref.5, f32[8,128]{1,0:T(8,128)} %fri_ref.5, f32[8,128]{1,0:T(8,128)} %load_ref.5, f32[4,2048,128]{2,1,0:T(8,128)} %bitcast.1), custom_call_target="tpu_custom_call" | custom-call | tf_op jit(solution)/shard_map/ask/pallas_call | solution.py:148
  34.2 58.0 %spread.1 = (f32[8,16,32,128]{3,2,1,0:T(8,128)}, f32[8,32,128]{2,1,0:T(8,128)}, f32[4,768,128]{2,1,0:T(8,128)}) custom-call(s32[3,96]{1,0:T(4,128)} %inter_rows.3, s32[3,96]{1,0:T(4,128)} %inter_rows.3, s32[1]{0:T(128)S(6)} %copy.8.length_ref, f32[8,3,16,128]{3,2,1,0:T(8,128)} %get-tuple-element.11.table_ref, ...), custom_call_target="tpu_custom_call" | custom-call | tf_op jit(solution)/shard_map/spread/pallas_call | solution.py:443
  92.2 21.0 %finish.1 = f32[8,96,128]{2,1,0:T(8,128)} custom-call(s32[3,96]{1,0:T(4,128)} %inter_rows.3, s32[3,96]{1,0:T(4,128)} %inter_rows.3, s32[1]{0:T(128)S(6)} %copy.8.length_ref, f32[8,16,32,128]{3,2,1,0:T(8,128)} %get-tuple-element.14.got_hbm, bf16[4,3072,256]{2,1,0:T(8,128)(2,1)} %get-tuple-element.12.weight_hbm, f32[4,768,128]{2,1,0:T(8,128)} %get-tuple-element.15.early_ref, ...), custom_call_target="tpu_custom_call" | custom-call | tf_op jit(solution)/shard_map/finish/pallas_call | solution.py:566
  113.2 1.8 %copy.9 = f32[8,96,128]{2,1,0:T(8,128)} copy(f32[8,96,128]{2,1,0:T(8,128)} %finish.1) | data formatting | bytes 786432

commit v3 on v2

v3 whole, which is shorter than its diff:
```python
import functools

import jax
import jax.numpy as jnp
from jax import lax
from jax.experimental import pallas as pl
from jax.experimental.pallas import tpu as pltpu
from jax.sharding import PartitionSpec as P

MESH = pl.DeviceIdType.MESH
F32 = jnp.float32
BF16 = jnp.bfloat16

PE = 128
LAGS = 16
BLOCK = 32
PATCH = 8
KER = 4
ENT = 24
NENT = KER * ENT
GRP = 8
SRC = 4
DAMP = 0.5
VMEM_LIMIT = 56 * 1024 * 1024
WIDE = 3 * LAGS * PE // 2
HALF = BLOCK // 2
PAD = 6


def recip(x):
    r = pl.reciprocal(x, approx=True)
    return r * (2.0 - x * r)


def newton(drive, friction, start=None):
    size = jnp.abs(drive) if start is None else drive
    v = size * (recip(DAMP + friction) if start is None else start)
    for _ in range(3):
        square = 1.0 + v * v
        root = lax.rsqrt(square)
        arc = jnp.log(v + square * root)
        v = (size + friction * (root * v - arc)) * recip(DAMP + friction * root)
    return jnp.where(drive < 0, -v, v) if start is None else v


def split(value):
    high = value.astype(BF16)
    return high, (value - high.astype(F32)).astype(BF16)


def history_of(k, rows):
    pre, fri, load, delay = rows[k, 0], rows[k, 1], rows[k, 2], rows[k, 3]
    start = recip(DAMP + fri)

    def history(ahead):
        time = lax.convert_element_type(ahead, F32) - delay
        v = newton(pre + load * (time + 1.0), fri, start)
        return jnp.where((time >= 0.0) & (time < 32.0), v, 0.0)

    return history


def put(k, high_ref, low_ref, start, left, right):
    at = pl.ds(pl.multiple_of(start, 2 * ENT), 2 * ENT)
    high_ref[k, at, 0:PE], low_ref[k, at, 0:PE] = split(left)
    high_ref[k, at, PE : 2 * PE], low_ref[k, at, PE : 2 * PE] = split(right)


def conv(k, half, offset, skip, high_ref, low_ref, weight_ref, carry_ref, terms):
    def stacked(ref, t, times, pairs):
        starts = [(t + 14 - 2 * j - offset) * ENT for j in pairs]
        return jnp.concatenate([ref[k, start : start + times * ENT, :] for start in starts], axis=1)

    base = LAGS * PE
    if half:
        carry = carry_ref[k]
    elif skip:
        carry = jnp.zeros((2 * ENT, PE), F32)
    else:
        rest = jnp.dot(stacked(low_ref, -2, 2, (0, 2, 4, 6)), weight_ref[k, base:, :], preferred_element_type=F32)
        carry = rest[:, PE:]
    for t in range(half * HALF, half * HALF + HALF, 8):
        pairs = [j for j in range(8) if not skip or 2 * j <= t + 7]
        evens = pairs[::2]
        both = jnp.dot(stacked(high_ref, t, 8, pairs), weight_ref[k, 0 : len(pairs) * 2 * PE, :], preferred_element_type=F32)
        rest = jnp.dot(
            stacked(low_ref, t, 8, evens), weight_ref[k, base : base + len(evens) * 2 * PE, :], preferred_element_type=F32
        )
        late = jnp.concatenate([carry, rest[: 6 * ENT, PE:]], axis=0)
        carry = rest[6 * ENT :, PE:]
        terms[k, t * ENT : (t + 8) * ENT, :] = both[:, :PE] + both[:, PE:] + (rest[:, :PE] + late)
    if not half:
        carry_ref[k] = carry


def routes(inter_ref, length):
    me = lax.axis_index("recv")
    shape = (SRC * PATCH, NENT)
    hit = jnp.broadcast_to(inter_ref[0:1, :], shape) == lax.broadcasted_iota(jnp.int32, shape, 0) + me * (SRC * PATCH)
    live = lax.broadcasted_iota(jnp.int32, shape, 1) < length
    return jnp.where(hit & live, 1.0, 0.0).astype(BF16)


def route(half, route_ref, terms, part_ref):
    def pair(i, carry):
        t = half * HALF + 2 * i
        rows = [
            jnp.concatenate([terms[k, pl.ds(pl.multiple_of((t + j) * ENT, 8), ENT), :] for k in range(KER)], axis=0)
            for j in range(2)
        ]
        high, low = split(jnp.concatenate(rows, axis=1))
        both = jnp.dot(route_ref[...], high, preferred_element_type=F32)
        both = both + jnp.dot(route_ref[...], low, preferred_element_type=F32)
        part_ref[pl.ds(2 * i, SRC * PATCH, stride=HALF), :] = both[:, :PE]
        part_ref[pl.ds(2 * i + 1, SRC * PATCH, stride=HALF), :] = both[:, PE:]
        return carry

    lax.fori_loop(0, HALF // 2, pair, 0, unroll=2)


def start_strips(part_ref, parts, send, recv):
    me, y = lax.axis_index("recv"), lax.axis_index("src")
    rows = PATCH * HALF
    copies = []
    for dy in (2, 1, 3):
        to = (y + dy) % SRC
        copies.append(
            pltpu.make_async_remote_copy(
                src_ref=part_ref.at[pl.ds(to * rows, rows)], dst_ref=parts.at[dy - 1],
                send_sem=send.at[dy - 1], recv_sem=recv.at[dy - 1],
                device_id=(me, to), device_id_type=MESH,
            )
        )
        copies[-1].start()
    return copies


def strip_sum(p, part_ref, parts):
    y = lax.axis_index("src")
    own = part_ref[pl.ds(pl.multiple_of((y * PATCH + p) * HALF, HALF), HALF), :]
    at = pl.ds(pl.multiple_of(p * HALF, HALF), HALF)
    return own + parts[0, at, :] + parts[1, at, :] + parts[2, at, :]


def solve_patch(p, time, count, stress, pre_ref, fri_ref, load_ref):
    pre, fri, load = pre_ref[pl.ds(p, 1), :], fri_ref[pl.ds(p, 1), :], load_ref[pl.ds(p, 1), :]
    times = lax.broadcasted_iota(jnp.int32, (count, PE), 0).astype(F32) + float(time + 1)
    drive = pre + load * times
    if stress is not None:
        drive = drive + stress
    return newton(drive, jnp.broadcast_to(fri, (count, PE)))


PEERS = (4, 3, 5, 2, 6, 7, 1)
CUTS = 2
STEP = 4


def rupture_kernel(
    n_z, inter_ref, inter_rows, length_ref, pre_ref, fri_ref, load_ref, kern_ref, out_ref,
    zbuf, req, wanted_ref, asked, chosen, table_ref, kern_f32, early_ref, got_ref, line,
    rows, weight, high, low, carry_ref, terms, route_ref, picked, *rest
):
    half, quarter = n_z // 2, n_z // STEP
    part, parts, own, rest = rest[0:4], rest[4:8], rest[8:10], rest[10:]
    right = {s: rest[2 * s - 2 : 2 * s] for s in range(1, half)}
    left = {s: rest[2 * (half + s) - 4 : 2 * (half + s) - 2] for s in range(1, half)}
    far = rest[4 * half - 4 : 4 * half - 2]
    req_s, req_r, z_s, z_r, ask_s, ask_r, y_s, y_r, r_s, r_r, l_s, l_r, x_s, x_r, loc = rest[4 * half - 2 :]
    right[half] = left[half] = far
    right[0] = left[0] = own
    me, y = lax.axis_index("recv"), lax.axis_index("src")
    z, k_me = me // GRP, me % GRP

    def at_z(dz):
        return (((z + dz + n_z) % n_z) * GRP + k_me, y)

    to_right, to_left = at_z(1), at_z(-1)
    barrier = pltpu.get_barrier_semaphore()
    for dy in range(1, SRC):
        pl.semaphore_signal(barrier, inc=1, device_id=(me, (y + dy) % SRC), device_id_type=MESH)
    for dz in (*range(STEP, n_z, STEP), 1, -1, -2):
        pl.semaphore_signal(barrier, inc=1, device_id=at_z(dz), device_id_type=MESH)
    for dk in range(1, GRP):
        pl.semaphore_signal(barrier, inc=1, device_id=(z * GRP + (k_me + dk) % GRP, y), device_id_type=MESH)
    fetch = pltpu.make_async_copy(kern_ref, kern_f32, loc.at[0])
    fetch.start()

    mine_at = (z % STEP) * quarter + z // STEP
    zbuf[mine_at, 0:8, :] = pre_ref[...]
    zbuf[mine_at, 8:16, :] = fri_ref[...]
    zbuf[mine_at, 16:24, :] = load_ref[...]
    row = inter_rows[1:2, :]
    eye = lax.broadcasted_iota(jnp.int32, (NENT, NENT), 0) == lax.broadcasted_iota(jnp.int32, (NENT, NENT), 1)
    column = jnp.sum(jnp.where(eye, jnp.broadcast_to(row, (NENT, NENT)), 0), axis=1, keepdims=True)
    owner_of = lax.shift_right_logical(column, 5)
    place_of = jnp.bitwise_and(column, PATCH - 1)
    hit = owner_of == lax.broadcasted_iota(jnp.int32, (NENT, n_z * GRP), 1)
    wanted = jnp.max(jnp.where(hit, place_of, 0), axis=0, keepdims=True)
    req[k_me] = jnp.broadcast_to(wanted, (8, n_z * GRP))
    route_ref[...] = routes(inter_rows, length_ref[0])

    def clear(k, carry):
        got_ref[k, :, 0:HALF, :] = jnp.zeros((n_z, HALF, PE), F32)
        return carry

    lax.fori_loop(0, GRP, clear, 0)
    pl.semaphore_wait(barrier, SRC - 1 + quarter - 1 + 3 + GRP - 1)

    def params(at, i, to):
        copy = pltpu.make_async_remote_copy(
            src_ref=zbuf.at[at], dst_ref=zbuf.at[at], send_sem=z_s.at[i], recv_sem=z_r.at[i],
            device_id=to, device_id_type=MESH,
        )
        copy.start()
        return copy

    near = [params(pl.ds(mine_at, 1), i - 1, at_z(i * STEP)) for i in sorted(range(1, quarter), key=lambda i: -min(i, quarter - i))]
    sends = []
    for dk in range(1, GRP):
        sends.append(
            pltpu.make_async_remote_copy(
                src_ref=req.at[k_me], dst_ref=req.at[k_me], send_sem=req_s.at[dk - 1], recv_sem=req_r.at[dk - 1],
                device_id=(z * GRP + (k_me + dk) % GRP, y), device_id_type=MESH,
            )
        )
        sends[-1].start()

    def weights(k, carry):
        for lag in range(LAGS):
            up, down = split(kern_f32[k, pl.ds(lag, PE, stride=LAGS), :].T)
            weight[k, lag * PE : (lag + 1) * PE, 0:PE] = up
            weight[k, lag * PE : (lag + 1) * PE, PE : 2 * PE] = down
            pair = lag // 2
            at, side = LAGS * PE + (pair // 2 * 2 + lag % 2) * PE, (pair % 2) * PE
            weight[k, at : at + PE, side : side + PE] = up
        return carry

    for copy in near:
        copy.wait_recv()
    group = pl.ds((z % STEP) * quarter, quarter)
    others = [params(group, quarter - 1 + i, at_z(dz)) for i, dz in enumerate((2, 1, -1))]
    fetch.wait()
    lax.fori_loop(0, KER, weights, 0)
    for copy in sends:
        copy.wait()
    for k in range(GRP):
        wanted_ref[k : k + 1, :] = req[k, 0:1, :]
    fall = pltpu.make_async_copy(wanted_ref, asked, loc.at[1])
    fall.start()
    fall.wait()
    for copy in others:
        copy.wait()
    for copy in near:
        copy.wait_send()

    def choose(k, carry):
        for zz in range(n_z):
            p = asked[k, zz * GRP + k_me]
            for i in range(3):
                chosen[k, i, zz : zz + 1, :] = zbuf[(zz % STEP) * quarter + zz // STEP, pl.ds(8 * i + p, 1), :]
        return carry

    lax.fori_loop(0, GRP, choose, 0)
    xsends = []
    for dk in PEERS:
        k = (k_me + dk) % GRP
        xsends.append(
            pltpu.make_async_remote_copy(
                src_ref=chosen.at[k], dst_ref=table_ref.at[k_me], send_sem=ask_s.at[dk - 1], recv_sem=ask_r.at[dk - 1],
                device_id=(z * GRP + k, y), device_id_type=MESH,
            )
        )
        xsends[-1].start()
    table_ref[k_me] = chosen[k_me]

    def known(p, carry):
        out_ref[p, 0:BLOCK] = solve_patch(p, 0, BLOCK, None, pre_ref, fri_ref, load_ref)
        return carry

    lax.fori_loop(0, PATCH, known, 0)
    for copy in xsends:
        copy.wait()

    for k in range(KER):
        high[k, 0 : PAD * ENT, :] = jnp.zeros((PAD * ENT, 2 * PE), BF16)
        low[k, 0 : PAD * ENT, :] = jnp.zeros((PAD * ENT, 2 * PE), BF16)

        def fill(e, carry):
            owner = lax.shift_right_logical(inter_ref[1, k * ENT + e], 5)
            zz, kk = owner // GRP, owner % GRP
            for i in range(3):
                rows[k, i, pl.ds(e, 1), :] = table_ref[kk, i, pl.ds(zz, 1), :]
            delay = inter_ref[2, k * ENT + e]
            rows[k, 3, pl.ds(e, 1), :] = jnp.full((1, PE), delay, jnp.int32).astype(F32)
            return carry

        lax.fori_loop(0, ENT, fill, 0, unroll=8)
        history = history_of(k, rows)

        def pair(i, before):
            now, after = history(32 + 2 * i), history(33 + 2 * i)
            side = jnp.concatenate([now, after], axis=0)
            put(k, high, low, (PAD + 2 * i) * ENT, side, jnp.concatenate([before, now], axis=0))
            return after

        lax.fori_loop(0, 16, pair, jnp.zeros((ENT, PE), F32))

    strips = []
    for th in range(2):
        for k in range(KER):
            conv(k, th, 14 - PAD, True, high, low, weight, carry_ref, terms)
        route(th, route_ref, terms, part[th])
        strips.append(start_strips(part[th], parts[th], y_s.at[th], y_r.at[th]))

    moves = {}

    def forward(s, th, h):
        for name, bufs, send, recv, to in (("r", right, r_s, r_r, to_right), ("l", left, l_s, l_r, to_left)):
            if s < half or (s == half and (h < CUTS // 2) == (name == "r")):
                at = pl.ds(h * (PATCH // CUTS), PATCH // CUTS)
                moves[name, s, th, h] = pltpu.make_async_remote_copy(
                    src_ref=bufs[s - 1][th].at[at], dst_ref=bufs[s][th].at[at],
                    send_sem=send.at[s - 1, th * CUTS + h], recv_sem=recv.at[s - 1, th * CUTS + h],
                    device_id=to, device_id_type=MESH,
                )
                moves[name, s, th, h].start()

    def pick(origin, slot, buffers):
        for k in range(GRP):
            for th in range(2):
                picked[k, slot, th * HALF : (th + 1) * HALF] = buffers[th][asked[k, origin * GRP + k_me]]

    def to_peers(first, count):
        for dk in PEERS:
            k = (k_me + dk) % GRP
            pltpu.make_async_remote_copy(
                src_ref=picked.at[k, pl.ds(first, count)], dst_ref=got_ref.at[k_me, pl.ds(first, count), pl.ds(HALF, BLOCK)],
                send_sem=x_s.at[dk - 1], recv_sem=x_r.at[dk - 1],
                device_id=(z * GRP + k, y), device_id_type=MESH,
            ).start()

    def early(i):
        def one(k, carry):
            history = history_of(k, rows)
            for b in range(4 * i, 4 * i + 4, 2):
                early_ref[k, b * ENT : (b + 2) * ENT, :] = jnp.concatenate([history(b + 48), history(b + 49)], axis=0)
            return carry

        lax.fori_loop(0, KER, one, 0)

    for th in range(2):
        for copy in strips[th]:
            copy.wait_recv()

        def solve(p, carry):
            v = solve_patch(p, BLOCK + th * HALF, HALF, strip_sum(p, part[th], parts[th]), pre_ref, fri_ref, load_ref)
            own[th][p] = v
            out_ref[p, BLOCK + th * HALF : BLOCK + (th + 1) * HALF] = v
            return carry

        lax.fori_loop(0, PATCH, solve, 0)
        for h in range(CUTS):
            forward(1, th, h)
    pick(z, 0, own)
    to_peers(0, 1)
    for s in range(1, half + 1):
        early(s - 1)
        for th in range(2):
            for h in range(CUTS):
                for name in "rl":
                    if (name, s, th, h) in moves:
                        moves[name, s, th, h].wait_recv()
                forward(s + 1, th, h)
        if s < half:
            pick((z + n_z - s) % n_z, 2 * s - 1, right[s])
            pick((z + s) % n_z, 2 * s, left[s])
            to_peers(2 * s - 1, 2)
        else:
            pick((z + half) % n_z, n_z - 1, far)
            to_peers(n_z - 1, 1)
    mine = pltpu.make_async_copy(picked.at[k_me], got_ref.at[k_me, :, pl.ds(HALF, BLOCK)], loc.at[2])
    mine.start()
    for dk in range(1, GRP):
        k = (k_me + dk) % GRP
        pltpu.make_async_remote_copy(
            src_ref=picked.at[k], dst_ref=got_ref.at[k_me, :, pl.ds(HALF, BLOCK)], send_sem=x_s.at[dk - 1], recv_sem=x_r.at[dk - 1],
            device_id=(z * GRP + k, y), device_id_type=MESH,
        ).wait()
    mine.wait()

    for k in range(KER):
        line[0 : 32 * ENT, :] = early_ref[k]
        line[32 * ENT : 48 * ENT, :] = jnp.zeros((16 * ENT, PE), F32)

        def place(e, carry):
            owner = lax.shift_right_logical(inter_ref[1, k * ENT + e], 5)
            delay = inter_ref[2, k * ENT + e]
            ahead = (owner // GRP - z + n_z) % n_z
            slot = jnp.where(ahead < n_z // 2, 2 * ahead, 2 * (n_z - ahead) - 1)
            line[pl.ds(16 * ENT + e, BLOCK, stride=ENT), :] += got_ref[owner % GRP, slot, pl.ds(jnp.clip(48 - delay, 0, HALF), BLOCK), :]
            return carry

        lax.fori_loop(0, ENT, place, 0, unroll=8)

        def pair(i, carry):
            left = line[pl.ds(pl.multiple_of((2 * i + 2) * ENT, 2 * ENT), 2 * ENT), :]
            right = line[pl.ds(pl.multiple_of((2 * i + 1) * ENT, ENT), 2 * ENT), :]
            put(k, high, low, 2 * i * ENT, left, right)
            return carry

        lax.fori_loop(0, 23, pair, 0)

    for th in range(2):
        for k in range(KER):
            conv(k, th, 0, False, high, low, weight, carry_ref, terms)
        route(th, route_ref, terms, part[2 + th])
        strips.append(start_strips(part[2 + th], parts[2 + th], y_s.at[2 + th], y_r.at[2 + th]))
    for th in range(2):
        for copy in strips[2 + th]:
            copy.wait_recv()

        def solve(p, carry):
            at = pl.ds(2 * BLOCK + th * HALF, HALF)
            stress = strip_sum(p, part[2 + th], parts[2 + th])
            out_ref[p, at] = solve_patch(p, 2 * BLOCK + th * HALF, HALF, stress, pre_ref, fri_ref, load_ref)
            return carry

        lax.fori_loop(0, PATCH, solve, 0)
    for copy in moves.values():
        copy.wait_send()
    for group in strips:
        for copy in group:
            copy.wait_send()


def local(interactions, list_lengths, kernels, prestress, friction, load_rate):
    n_z = lax.axis_size("recv") // GRP
    half = n_z // 2
    owners = n_z * GRP
    vm = pl.BlockSpec(memory_space=pltpu.VMEM)
    sm = pl.BlockSpec(memory_space=pltpu.SMEM)
    dma = pltpu.SemaphoreType.DMA
    part = pltpu.VMEM((SRC * PATCH * HALF, PE), F32)
    parts = pltpu.VMEM((SRC - 1, PATCH * HALF, PE), F32)
    halves = pltpu.VMEM((PATCH, HALF, PE), F32)
    peers = dma((GRP - 1,))
    return pl.pallas_call(
        functools.partial(rupture_kernel, n_z),
        out_shape=jax.ShapeDtypeStruct((PATCH, 3 * BLOCK, PE), F32),
        in_specs=[sm, vm, sm, vm, vm, vm, pl.BlockSpec(memory_space=pl.ANY)],
        out_specs=vm,
        scratch_shapes=[
            pltpu.VMEM((n_z, 24, PE), F32),
            pltpu.VMEM((GRP, 8, owners), jnp.int32),
            pltpu.VMEM((GRP, owners), jnp.int32),
            pltpu.SMEM((GRP, owners), jnp.int32),
            pltpu.VMEM((GRP, 3, n_z, PE), F32),
            pltpu.VMEM((GRP, 3, n_z, PE), F32),
            pltpu.VMEM((KER, LAGS * PE, PE), F32),
            pltpu.VMEM((KER, BLOCK * ENT, PE), F32),
            pltpu.VMEM((GRP, n_z, HALF + BLOCK, PE), F32),
            pltpu.VMEM((48 * ENT, PE), F32),
            pltpu.VMEM((KER, 4, ENT, PE), F32),
            pltpu.VMEM((KER, WIDE, 2 * PE), BF16),
            pltpu.VMEM((KER, 46 * ENT, 2 * PE), BF16),
            pltpu.VMEM((KER, 46 * ENT, 2 * PE), BF16),
            pltpu.VMEM((KER, 2 * ENT, PE), F32),
            pltpu.VMEM((KER, BLOCK * ENT, PE), F32),
            pltpu.VMEM((SRC * PATCH, NENT), BF16),
            pltpu.VMEM((GRP, n_z, BLOCK, PE), F32),
            part, part, part, part, parts, parts, parts, parts,
            *[halves for _ in range(2 + 2 * (2 * (half - 1) + 1))],
            peers, peers, dma((n_z // STEP + 2,)), dma((n_z // STEP + 2,)), peers, peers,
            dma((4, SRC - 1)), dma((4, SRC - 1)),
            *[dma((half, 2 * CUTS)) for _ in range(4)],
            peers, peers, dma((3,)),
        ],
        compiler_params=pltpu.CompilerParams(
            collective_id=0, has_side_effects=True, vmem_limit_bytes=VMEM_LIMIT
        ),
        name="rupture",
    )(interactions, interactions, list_lengths, prestress, friction, load_rate, kernels.reshape(KER, PE * LAGS, PE))


def solution(mesh):
    own = P(("recv", "src"))
    in_specs = (
        P(None, ("recv", "src")),
        own,
        P(("recv", "src"), None, None, None),
        P(("recv", "src"), None),
        P(("recv", "src"), None),
        P(("recv", "src"), None),
    )
    out_specs = P(("recv", "src"), None, None)
    return jax.shard_map(local, mesh=mesh, in_specs=in_specs, out_specs=out_specs, check_vma=False)
```

time: 115 us -> 105 us (0.913)
  Pallas kernels: 113 us -> 103 us
    pallas_call x3 -> x1, Pallas kernels: 113 us -> 103 us  [local(): pl.pallas_call(functools.partial(rupture_kernel, n_z), out_shape=jax.Shap...]
where the time goes in v3:
time: 105 us
  Pallas kernels  103 us (98%)
  local copies, waits for them, and re-layouts  1.77 us (2%)
    pallas_call x1, Pallas kernels, local(): pl.pallas_call(functools.partial(rupture_kernel, n_z), out_shape=jax.Shap...  103 us

profile of v3, /device:TPU:1, one launch (start us, length us, event | category | flops | bytes accessed | tf_op | source)
XLA Modules:
  0.0 105.2 jit_solution(7049586643817503440)
XLA Ops:
  0.7 102.7 %rupture.1 = f32[8,96,128]{2,1,0:T(8,128)} custom-call(s32[3,96]{1,0:T(4,128)} %inter_rows.1, s32[3,96]{1,0:T(4,128)} %inter_rows.1, s32[1]{0:T(128)S(6)} %copy.8.length_ref, f32[8,128]{1,0:T(8,128)} %pre_ref.1, f32[8,128]{1,0:T(8,128)} %fri_ref.1, f32[8,128]{1,0:T(8,128)} %load_ref.1, f32[4,2048,128]{2,1,0:T(8,128)} %bitcast.1), custom_call_target="tpu_custom_call" | custom-call | tf_op jit(solution)/shard_map/rupture/pallas_call | solution.py:448
  103.4 1.8 %copy.9 = f32[8,96,128]{2,1,0:T(8,128)} copy(f32[8,96,128]{2,1,0:T(8,128)} %rupture.1) | data formatting | bytes 786432

commit v4 on v3

--- a/solution.py
+++ b/solution.py
@@ -158,7 +158,7 @@
 
 def rupture_kernel(
     n_z, inter_ref, inter_rows, length_ref, pre_ref, fri_ref, load_ref, kern_ref, out_ref,
-    zbuf, req, wanted_ref, asked, chosen, table_ref, kern_f32, early_ref, got_ref, line,
+    zbuf, req, wanted_ref, asked, chosen, table_ref, kern_f32, early_ref, got_ref,
     rows, weight, high, low, carry_ref, terms, route_ref, picked, *rest
 ):
     half, quarter = n_z // 2, n_z // STEP
@@ -362,10 +362,20 @@
         lax.fori_loop(0, PATCH, solve, 0)
         for h in range(CUTS):
             forward(1, th, h)
+    def line_up(k, i, carry):
+        left = early_ref[k, pl.ds(pl.multiple_of((2 * i + 2) * ENT, 2 * ENT), 2 * ENT), :]
+        right = early_ref[k, pl.ds(pl.multiple_of((2 * i + 1) * ENT, ENT), 2 * ENT), :]
+        put(k, high, low, 2 * i * ENT, left, right)
+        return carry
+
     pick(z, 0, own)
     to_peers(0, 1)
     for s in range(1, half + 1):
         early(s - 1)
+        if s > half - KER:
+            k = s - (half - KER) - 1
+            early_ref[k, 32 * ENT :, :] = jnp.zeros((16 * ENT, PE), F32)
+            lax.fori_loop(0, 7, functools.partial(line_up, k), 0)
         for th in range(2):
             for h in range(CUTS):
                 for name in "rl":
@@ -390,26 +400,17 @@
     mine.wait()
 
     for k in range(KER):
-        line[0 : 32 * ENT, :] = early_ref[k]
-        line[32 * ENT : 48 * ENT, :] = jnp.zeros((16 * ENT, PE), F32)
-
         def place(e, carry):
             owner = lax.shift_right_logical(inter_ref[1, k * ENT + e], 5)
             delay = inter_ref[2, k * ENT + e]
             ahead = (owner // GRP - z + n_z) % n_z
             slot = jnp.where(ahead < n_z // 2, 2 * ahead, 2 * (n_z - ahead) - 1)
-            line[pl.ds(16 * ENT + e, BLOCK, stride=ENT), :] += got_ref[owner % GRP, slot, pl.ds(jnp.clip(48 - delay, 0, HALF), BLOCK), :]
+            early_ref[k, pl.ds(16 * ENT + e, BLOCK, stride=ENT), :] += got_ref[owner % GRP, slot, pl.ds(jnp.clip(48 - delay, 0, HALF), BLOCK), :]
             return carry
 
         lax.fori_loop(0, ENT, place, 0, unroll=8)
 
-        def pair(i, carry):
-            left = line[pl.ds(pl.multiple_of((2 * i + 2) * ENT, 2 * ENT), 2 * ENT), :]
-            right = line[pl.ds(pl.multiple_of((2 * i + 1) * ENT, ENT), 2 * ENT), :]
-            put(k, high, low, 2 * i * ENT, left, right)
-            return carry
-
-        lax.fori_loop(0, 23, pair, 0)
+        lax.fori_loop(7, 23, functools.partial(line_up, k), 0)
 
     for th in range(2):
         for k in range(KER):
@@ -458,9 +459,8 @@
             pltpu.VMEM((GRP, 3, n_z, PE), F32),
             pltpu.VMEM((GRP, 3, n_z, PE), F32),
             pltpu.VMEM((KER, LAGS * PE, PE), F32),
-            pltpu.VMEM((KER, BLOCK * ENT, PE), F32),
+            pltpu.VMEM((KER, 48 * ENT, PE), F32),
             pltpu.VMEM((GRP, n_z, HALF + BLOCK, PE), F32),
-            pltpu.VMEM((48 * ENT, PE), F32),
             pltpu.VMEM((KER, 4, ENT, PE), F32),
             pltpu.VMEM((KER, WIDE, 2 * PE), BF16),
             pltpu.VMEM((KER, 46 * ENT, 2 * PE), BF16),

time: 105 us -> 105 us (level)
  no operation moved by 1% of the time
where the time goes in v4:
time: 105 us
  Pallas kernels  102 us (97%)
  local copies, waits for them, and re-layouts  1.77 us (2%)
    pallas_call x1, Pallas kernels, local(): pl.pallas_call(functools.partial(rupture_kernel, n_z), out_shape=jax.Shap...  102 us

profile of v4, /device:TPU:1, one launch (start us, length us, event | category | flops | bytes accessed | tf_op | source)
XLA Modules:
  0.0 104.6 jit_solution(17587112665500350985)
XLA Ops:
  0.7 102.2 %rupture.1 = f32[8,96,128]{2,1,0:T(8,128)} custom-call(s32[3,96]{1,0:T(4,128)} %inter_rows.1, s32[3,96]{1,0:T(4,128)} %inter_rows.1, s32[1]{0:T(128)S(6)} %copy.8.length_ref, f32[8,128]{1,0:T(8,128)} %pre_ref.1, f32[8,128]{1,0:T(8,128)} %fri_ref.1, f32[8,128]{1,0:T(8,128)} %load_ref.1, f32[4,2048,128]{2,1,0:T(8,128)} %bitcast.1), custom_call_target="tpu_custom_call" | custom-call | tf_op jit(solution)/shard_map/rupture/pallas_call | solution.py:449
  102.9 1.8 %copy.9 = f32[8,96,128]{2,1,0:T(8,128)} copy(f32[8,96,128]{2,1,0:T(8,128)} %rupture.1) | data formatting | bytes 786432
